TPU v7x, 32 devices: a whole 2x2x4 slice. The times are simulated.
32 devices in a mesh: ctx: 8 (over z, x), head: 4 (over y, core).
Axes of the slice: x: 2, y: 2, z: 4, core: 2. Of those that a mesh axis runs over, the one named last changes fastest.
Arguments:
- queries: bfloat16 [8192, 1024], P(('ctx', 'head')), may hold values from -6 to 6
- keys: bfloat16 [8192, 1024], P(('ctx', 'head')), may hold values from -6 to 6
- values: bfloat16 [8192, 1024], P(('ctx', 'head')), may hold values from -6 to 6
- grads_out: bfloat16 [8192, 1024], P(('ctx', 'head')), may hold values from -6 to 6
- log_decay: float32 [8, 8192], P('head', 'ctx'), may hold values from -0.8 to 0
- ridge: float32 [8], P('head'), may hold values from 0.25 to 2
Outputs:
- grad_queries: bfloat16 [8192, 1024], P(('ctx', 'head'))
- grad_keys: bfloat16 [8192, 1024], P(('ctx', 'head'))
- grad_values: bfloat16 [8192, 1024], P(('ctx', 'head'))
All inputs are finite; a program needn't handle non-finite values.
Results may differ from a plain program's by a relative error of at most 0.0085.
Values may be sent and summed in bfloat16 or wider, within the bound.
A program may use at most 128 MiB of HBM per device.

v0:
```python
import jax
import jax.numpy as jnp
from jax import lax
from jax.sharding import PartitionSpec as P

DH = 128
SPAN = 512
SOLVE_STEPS = 8


highest = lax.Precision.HIGHEST
epsilon = 1e-06


def product(left, right):
    return jnp.dot(
        left.astype(jnp.float32),
        right.astype(jnp.float32),
        precision=highest,
        preferred_element_type=jnp.float32,
    )


def mixed(left, right):
    return jnp.dot(left, right, preferred_element_type=jnp.float32)


def block_decays(log_gate):
    cumul = jnp.cumsum(log_gate)
    size = log_gate.shape[0]
    rowpos = lax.broadcasted_iota(jnp.int32, (size, size), 0)
    column_position = lax.broadcasted_iota(jnp.int32, (size, size), 1)
    within = jnp.exp(
        jnp.where(rowpos >= column_position, cumul[:, None] - cumul[None, :], -jnp.inf)
    )
    return (cumul, within)


def multiply_by_matrix(direction, gram, keys, within, start_decay, ridge):
    scores = (within * mixed(direction.astype(jnp.bfloat16), keys.T)).astype(jnp.bfloat16)
    return start_decay[:, None] * product(direction, gram) + mixed(scores, keys) + ridge * direction


def conj_grad(rhs, gram, keys, within, start_decay, ridge):
    solution = jnp.zeros_like(rhs)
    residual = rhs
    direction = rhs
    rho_now = jnp.sum(rhs * rhs, axis=-1, keepdims=True)
    for sweep in range(SOLVE_STEPS):
        image = multiply_by_matrix(direction, gram, keys, within, start_decay, ridge)
        step_size = rho_now / (jnp.sum(direction * image, axis=-1, keepdims=True) + epsilon)
        solution = solution + step_size * direction
        residual = residual - step_size * image
        rho_next = jnp.sum(residual * residual, axis=-1, keepdims=True)
        direction = residual + rho_next / (rho_now + epsilon) * direction
        rho_now = rho_next
    return solution


def span_solve(gram, value_state, queries, keys, values, grads_out, log_gate, ridge):
    cumul, within = block_decays(log_gate)
    start_decay = jnp.exp(cumul)
    solved = conj_grad(queries.astype(jnp.float32), gram, keys, within, start_decay, ridge)
    scores = (within * mixed(grads_out, values.T)).astype(jnp.bfloat16)
    rhs = start_decay[:, None] * product(grads_out, value_state) + mixed(scores, keys)
    adjoint = conj_grad(rhs, gram, keys, within, start_decay, ridge)
    return (solved, adjoint)


def span_grads(value_memory_state, state_gram, keys, values, grads_out, solved, adjoint, log_gate):
    cumul, within = block_decays(log_gate)
    end_weight = jnp.exp(cumul[-1] - cumul)[:, None]
    solved_low = solved.astype(jnp.bfloat16)
    adjoint_low = adjoint.astype(jnp.bfloat16)
    solved_along_keys = (within * mixed(solved_low, keys.T)).astype(jnp.bfloat16)
    along_adjoint = (within * mixed(adjoint_low, keys.T)).astype(jnp.bfloat16)
    along_values = (within * mixed(grads_out, values.T)).astype(jnp.bfloat16)
    grad_values = mixed(solved_along_keys.T, grads_out) + end_weight * product(
        keys, value_memory_state.T
    )
    grad_keys = mixed(along_values.T, solved_low) + end_weight * product(values, value_memory_state)
    grad_keys = (
        grad_keys - mixed(solved_along_keys.T, adjoint_low) - mixed(along_adjoint.T, solved_low)
    )
    grad_keys = grad_keys + end_weight * product(keys, state_gram + state_gram.T)
    return (grad_keys, grad_values)


def split_heads(block, head_dev):
    rows = block.shape[0]
    return block.reshape(rows // SPAN, SPAN, head_dev, DH).transpose(2, 0, 1, 3)


def join_heads(block):
    head_dev, count, size, width = block.shape
    return block.transpose(1, 2, 0, 3).reshape(count * size, head_dev * width).astype(jnp.bfloat16)


def scale_mats(factor, mats):
    return factor[..., None, None] * mats


def shards(queries, keys, values, grads_out, log_decay, ridge):
    gathered = (
        lax.all_to_all(queries, "head", split_axis=1, concat_axis=0, tiled=True),
        lax.all_to_all(keys, "head", split_axis=1, concat_axis=0, tiled=True),
        lax.all_to_all(values, "head", split_axis=1, concat_axis=0, tiled=True),
        lax.all_to_all(grads_out, "head", split_axis=1, concat_axis=0, tiled=True),
    )
    head_dev = log_decay.shape[0]
    query_h = split_heads(gathered[0], head_dev)
    key_h = split_heads(gathered[1], head_dev)
    value_h = split_heads(gathered[2], head_dev)
    grad_h = split_heads(gathered[3], head_dev)
    count = query_h.shape[1]
    gates = log_decay.reshape(head_dev, count, SPAN)
    sums = jnp.sum(gates, axis=2)
    through_local = jnp.cumsum(sums, axis=1)
    starts = jnp.concatenate([jnp.zeros_like(sums[:, :1]), through_local[:, :-1]], axis=1)
    total_log = jnp.sum(sums, axis=1)
    cumul = jnp.cumsum(gates, axis=2)
    key_wide = key_h.astype(jnp.float32)
    scaled_lookup_vectors = jnp.exp(cumul[..., -1:] - cumul)[..., None] * key_wide
    gram_parts = jnp.einsum("hnck,hncl->hnkl", key_wide, scaled_lookup_vectors, precision=highest)
    value_parts = jnp.einsum(
        "hncv,hnck->hnvk", value_h.astype(jnp.float32), scaled_lookup_vectors, precision=highest
    )
    zeros = jnp.zeros((head_dev, DH, DH), jnp.float32)
    gram_carry, value_carry = (zeros, zeros)
    gram_local, value_local = ([], [])
    for block in range(count):
        gram_local.append(gram_carry)
        value_local.append(value_carry)
        decay = jnp.exp(sums[:, block])
        gram_carry = scale_mats(decay, gram_carry) + gram_parts[:, block]
        value_carry = scale_mats(decay, value_carry) + value_parts[:, block]
    position = lax.axis_index("ctx")
    totals = lax.all_gather(total_log[None], "ctx", axis=0, tiled=True)
    through = jnp.cumsum(totals, axis=0)
    exclusive = jnp.concatenate([jnp.zeros_like(totals[:1]), through[:-1]], axis=0)
    mine_excl = lax.dynamic_slice_in_dim(exclusive, position, 1, 0)
    mine_through = lax.dynamic_slice_in_dim(through, position, 1, 0)
    piece = (
        lax.all_gather(gram_carry[None], "ctx", axis=0, tiled=True),
        lax.all_gather(value_carry[None], "ctx", axis=0, tiled=True),
    )
    number = piece[0].shape[0]
    index = jnp.arange(number, dtype=jnp.int32)
    gap = mine_excl - through
    weight = jnp.where((index < position)[:, None], jnp.exp(jnp.minimum(gap, 0.0)), 0.0)
    gram_in = jnp.einsum("jh,jhkl->hkl", weight, piece[0], precision=highest)
    value_in = jnp.einsum("jh,jhkl->hkl", weight, piece[1], precision=highest)
    entry = jnp.exp(starts)
    gram_start = scale_mats(entry, gram_in[:, None]) + jnp.stack(gram_local, axis=1)
    value_start = scale_mats(entry, value_in[:, None]) + jnp.stack(value_local, axis=1)
    solve_blocks = jax.vmap(
        jax.vmap(span_solve, in_axes=(0, 0, 0, 0, 0, 0, 0, None)), in_axes=(0, 0, 0, 0, 0, 0, 0, 0)
    )
    solved, adjoint = solve_blocks(
        gram_start, value_start, query_h, key_h, value_h, grad_h, gates, ridge
    )
    weighted_solved = jnp.exp(cumul)[..., None] * solved
    value_back = jnp.einsum(
        "hncv,hnck->hnvk", grad_h.astype(jnp.float32), weighted_solved, precision=highest
    )
    gram_back = -jnp.einsum("hnck,hncl->hnkl", adjoint, weighted_solved, precision=highest)
    value_delta = jnp.einsum("hn,hnvk->hvk", entry, value_back, precision=highest)
    gram_delta = jnp.einsum("hn,hnvk->hvk", entry, gram_back, precision=highest)
    piece = (
        lax.all_gather(value_delta[None].astype(jnp.bfloat16), "ctx", axis=0, tiled=True).astype(
            jnp.float32
        ),
        lax.all_gather(gram_delta[None].astype(jnp.bfloat16), "ctx", axis=0, tiled=True).astype(
            jnp.float32
        ),
    )
    number = piece[0].shape[0]
    index = jnp.arange(number, dtype=jnp.int32)
    gap = exclusive - mine_through
    weight = jnp.where((index > position)[:, None], jnp.exp(jnp.minimum(gap, 0.0)), 0.0)
    value_after = zeros + jnp.einsum("jh,jhkl->hkl", weight, piece[0], precision=highest)
    outer_product_suffix = zeros + jnp.einsum("jh,jhkl->hkl", weight, piece[1], precision=highest)
    value_next = [None] * count
    gram_next = [None] * count
    for block in reversed(range(count)):
        value_next[block] = value_after
        gram_next[block] = outer_product_suffix
        decay = jnp.exp(sums[:, block])
        value_after = scale_mats(decay, value_after) + value_back[:, block]
        outer_product_suffix = scale_mats(decay, outer_product_suffix) + gram_back[:, block]
    grad_blocks = jax.vmap(jax.vmap(span_grads))
    grad_keys, grad_values = grad_blocks(
        jnp.stack(value_next, axis=1),
        jnp.stack(gram_next, axis=1),
        key_h,
        value_h,
        grad_h,
        solved,
        adjoint,
        gates,
    )
    results = (
        lax.all_to_all(join_heads(adjoint), "head", split_axis=0, concat_axis=1, tiled=True),
        lax.all_to_all(join_heads(grad_keys), "head", split_axis=0, concat_axis=1, tiled=True),
        lax.all_to_all(join_heads(grad_values), "head", split_axis=0, concat_axis=1, tiled=True),
    )
    return (results[0], results[1], results[2])


def solution(mesh):
    return jax.shard_map(
        shards,
        mesh=mesh,
        in_specs=(
            P(("ctx", "head"), None),
            P(("ctx", "head"), None),
            P(("ctx", "head"), None),
            P(("ctx", "head"), None),
            P("head", "ctx"),
            P("head"),
        ),
        out_specs=(P(("ctx", "head"), None), P(("ctx", "head"), None), P(("ctx", "head"), None)),
        check_vma=False,
    )
```

profile of v0, /device:TPU:0, one launch (start us, length us, event | category | flops | bytes accessed | tf_op | source)
XLA Modules:
  0.0 427.7 jit_solution(12633840354365220931)
XLA Ops:
  9.1 4.2 all-to-all-start
  15.9 6.3 %all-to-all-done = bf16[256,4,256]{2,0,1:T(8,128)(2,1)S(1)} async-done(((bf16[256,4,256]{2,0,1:T(8,128)(2,1)}), bf16[256,4,256]{2,0,1:T(8,128)(2,1)S(1)}, u32[]{:S(2)}, u32[]{:S(2)}) %all-to-all-start) | async-done | bytes 524320 | tf_op jit(solution)/shard_map/all_to_all | solution.py:106
  27.9 6.6 %all-to-all-done.1 = bf16[256,4,256]{2,0,1:T(8,128)(2,1)S(1)} async-done(((bf16[256,4,256]{2,0,1:T(8,128)(2,1)}), bf16[256,4,256]{2,0,1:T(8,128)(2,1)S(1)}, u32[]{:S(2)}, u32[]{:S(2)}) %all-to-all-start.1) | async-done | bytes 524320 | tf_op jit(solution)/shard_map/all_to_all | solution.py:107
  42.9 22.4 %all-reduce.4 = f32[16]{0:T(128)S(1)} all-reduce(f32[16]{0:T(128)S(1)} %dynamic-update-slice), channel_id=2, replica_groups=mesh['ctx'=8,'head'=4] {'ctx'}, use_global_device_ids=true, to_apply=%add.4 | all-reduce | flops 16 | bytes 128
  74.2 6.0 %all-to-all-done.4 = bf16[256,4,256]{2,0,1:T(8,128)(2,1)S(1)} async-done(((bf16[256,4,256]{2,0,1:T(8,128)(2,1)}), bf16[256,4,256]{2,0,1:T(8,128)(2,1)S(1)}, u32[]{:S(2)}, u32[]{:S(2)}) %all-to-all-start.4) | async-done | bytes 524320 | tf_op jit(solution)/shard_map/all_to_all | solution.py:105
  86.9 32.4 %all-gather.6.cloned.1.call-done = f32[8,2,128,128]{3,2,1,0:T(8,128)} async-done(((f32[1,2,128,128]{3,2,1,0:T(8,128)}), f32[8,2,128,128]{3,2,1,0:T(8,128)}) %all-gather.6.cloned.1.call-update) | async-done | bytes 1048592 | tf_op jit(solution)/shard_map/all_gather | solution.py:145
  126.4 4.0 fusion.9
  134.8 4.0 fusion.10
  144.1 4.3 fusion.11
  154.1 4.3 fusion.12
  164.2 4.2 fusion.13
  174.1 4.5 %fusion.14 = f32[2,2,512,128]{2,3,1,0:T(8,128)} fusion(f32[2,2,512]{2,1,0:T(2,128)S(1)} %copy-done.65, pred[512,512]{1,0:T(8,128)(4,1)} %iota_compare_fusion, bf16[2,512,2,128]{1,3,0,2:T(8,128)(2,1)S(1)} %copy.325, f32[2,2,512,128]{2,3,1,0:T(8,128)} %multiply_add_fusion.2), kind=kOutput, calls=%fused_computation.40 | convolution fusion | flops 541327360 | bytes 2891776 | tf_op jit(solution)/shard_map/vmap(vmap())/dot_general | solution.py:25
  183.7 4.2 fusion.15
  191.2 4.1 broadcast_multiply_fusion
  202.7 3.5 multiply_reduce_fusion.30
  210.3 4.8 %multiply_reduce_fusion.28 = (f32[2,2,512]{2,1,0:T(2,128)S(1)}, f32[2,2,512,128]{2,3,1,0:T(8,128)}) fusion(f32[2,2,512,128]{2,3,1,0:T(8,128)S(1)} %multiply_add_fusion.19, f32[2]{0:T(128)S(1)} %copy-done.60, f32[2,2,512,128]{2,3,1,0:T(8,128)} %fusion.226, f32[2,2,512]{2,1,0:T(2,128)S(1)} %get-tuple-element.50, bf16[2,512,2,128]{1,3,0,2:T(8,128)(2,1)} %copy-done.46, ...), kind=kOutput, calls=%fused_computation.209 | convolution fusion | flops 542898176 | bytes 3956744 | tf_op jit(solution)/shard_map/vmap(vmap())/dot_general | solution.py:25
  220.5 4.7 %multiply_reduce_fusion.26 = (f32[2,2,512]{2,1,0:T(2,128)S(1)}, f32[2,2,512,128]{2,3,1,0:T(8,128)}) fusion(f32[2,2,512,128]{2,3,1,0:T(8,128)S(1)} %multiply_add_fusion.17, f32[2]{0:T(128)S(1)} %copy-done.60, f32[2,2,512,128]{2,3,1,0:T(8,128)} %fusion.224, f32[2,2,512]{2,1,0:T(2,128)S(1)} %get-tuple-element.50, bf16[2,512,2,128]{1,3,0,2:T(8,128)(2,1)} %copy-done.46, ...), kind=kOutput, calls=%fused_computation.204 | convolution fusion | flops 542898176 | bytes 3956744 | tf_op jit(solution)/shard_map/vmap(vmap())/dot_general | solution.py:25
  232.0 5.5 %multiply_reduce_fusion.24 = (f32[2,2,512]{2,1,0:T(2,128)S(1)}, f32[2,2,512,128]{2,3,1,0:T(8,128)}) fusion(f32[2,2,512,128]{2,3,1,0:T(8,128)} %copy-done, f32[2]{0:T(128)S(1)} %copy-done.60, f32[2,2,512,128]{2,3,1,0:T(8,128)} %fusion.222, f32[2,2,512]{2,1,0:T(2,128)S(1)} %get-tuple-element.50, bf16[2,512,2,128]{1,3,0,2:T(8,128)(2,1)} %copy-done.46, ...), kind=kOutput, calls=%fused_computation.199 | convolution fusion | flops 542898176 | bytes 3956744 | tf_op jit(solution)/shard_map/vmap(vmap())/dot_general | solution.py:25
  244.5 5.6 %multiply_reduce_fusion.22 = (f32[2,2,512]{2,1,0:T(2,128)S(1)}, f32[2,2,512,128]{2,3,1,0:T(8,128)}) fusion(f32[2,2,512,128]{2,3,1,0:T(8,128)} %copy-done.3, f32[2]{0:T(128)S(1)} %copy-done.60, f32[2,2,512,128]{2,3,1,0:T(8,128)} %fusion.220, f32[2,2,512]{2,1,0:T(2,128)S(1)} %get-tuple-element.50, bf16[2,512,2,128]{1,3,0,2:T(8,128)(2,1)} %copy-done.46, ...), kind=kOutput, calls=%fused_computation.194 | convolution fusion | flops 542898176 | bytes 3956744 | tf_op jit(solution)/shard_map/vmap(vmap())/dot_general | solution.py:25
  256.9 5.3 %multiply_reduce_fusion.20 = (f32[2,2,512]{2,1,0:T(2,128)S(1)}, f32[2,2,512,128]{2,3,1,0:T(8,128)}) fusion(f32[2,2,512,128]{2,3,1,0:T(8,128)} %copy-done.6, f32[2]{0:T(128)S(1)} %copy-done.60, f32[2,2,512,128]{2,3,1,0:T(8,128)} %fusion.218, f32[2,2,512]{2,1,0:T(2,128)S(1)} %get-tuple-element.50, bf16[2,512,2,128]{1,3,0,2:T(8,128)(2,1)} %copy-done.46, ...), kind=kOutput, calls=%fused_computation.189 | convolution fusion | flops 542898176 | bytes 3956744 | tf_op jit(solution)/shard_map/vmap(vmap())/dot_general | solution.py:25
  269.1 5.7 %multiply_reduce_fusion.18 = (f32[2,2,512]{2,1,0:T(2,128)S(1)}, f32[2,2,512,128]{2,3,1,0:T(8,128)}, f32[2,2,512,128]{2,3,1,0:T(8,128)}) fusion(f32[2,2,512,128]{2,3,1,0:T(8,128)} %copy-done.14, f32[2]{0:T(128)S(1)} %copy-done.60, f32[2,2,512,128]{2,3,1,0:T(8,128)} %fusion.216, f32[2,2,512]{2,1,0:T(2,128)S(1)} %get-tuple-element.50, ...), kind=kOutput, calls=%fused_computation.184 | convolution fusion | flops 542898176 | bytes 5005320 | tf_op jit(solution)/shard_map/vmap(vmap())/dot_general | solution.py:25
  280.2 4.5 %fusion.7 = f32[2,2,512,128]{2,3,1,0:T(8,128)} fusion(f32[2,2,512]{2,1,0:T(2,128)S(1)} %copy-done.67, pred[512,512]{1,0:T(8,128)(4,1)} %iota_compare_fusion, bf16[2,512,2,128]{1,3,0,2:T(8,128)(2,1)} %copy-done.46, f32[2,2,512,128]{2,3,1,0:T(8,128)} %multiply_add_fusion.7), kind=kOutput, calls=%fused_computation.33 | convolution fusion | flops 541327360 | bytes 2891776 | tf_op jit(solution)/shard_map/vmap(vmap())/dot_general | solution.py:25
  288.1 4.0 multiply_add_fusion
  292.0 4.8 %fusion.17 = f32[2,512,2,128]{3,1,0,2:T(8,128)} fusion(f32[2,2,512]{2,1,0:T(2,128)S(1)} %copy-done.68, pred[512,512]{1,0:T(8,128)(4,1)} %iota_compare_fusion, bf16[2,512,2,128]{1,3,0,2:T(8,128)(2,1)} %copy-done.46, f32[2,2,512,128]{2,3,1,0:T(8,128)} %multiply_add_fusion, bf16[2,2,512,128]{2,3,1,0:T(8,128)(2,1)} %copy-done.51), kind=kOutput, calls=%fused_computation.46 | convolution fusion | flops 541327360 | bytes 3416064 | tf_op jit(solution)/shard_map/vmap(vmap())/dot_general | solution.py:25
  301.8 6.1 %fusion.68 = bf16[2,512,2,128]{1,3,0,2:T(8,128)(2,1)} fusion(f32[2,2,512,128]{2,3,1,0:T(8,128)} %get-tuple-element.72, f32[2,2,512,128]{2,3,1,0:T(8,128)} %fusion.216, f32[2,2,512,128]{2,3,1,0:T(8,128)} %get-tuple-element.71, f32[2,2,512,128]{2,3,1,0:T(8,128)} %fusion.218, f32[2,2,512,128]{2,3,1,0:T(8,128)} %get-tuple-element.69, ...), kind=kLoop, calls=%fused_computation.114 | loop fusion | flops 19398656 | bytes 17432584 | tf_op jit(solution)/shard_map/convert_element_type | solution.py:96
  310.5 4.4 %all-to-all-start.3 = ((bf16[4,256,256]{2,1,0:T(8,128)(2,1)}), bf16[4,256,256]{2,1,0:T(8,128)(2,1)}, u32[]{:S(2)}, u32[]{:S(2)}) async-start(bf16[4,256,256]{2,1,0:T(8,128)(2,1)} %convert_element_type.176), calls=%async_computation.3 | async-start | bytes 1048576 | tf_op jit(solution)/shard_map/all_to_all | solution.py:203
  315.0 3.5 convolution_bitcast_fusion.1
  319.7 31.3 %all-gather.2 = bf16[16,128,128]{2,1,0:T(8,128)(2,1)S(1)} all-gather(bf16[2,128,128]{2,1,0:T(8,128)(2,1)S(1)} %convert_element_type.199), channel_id=4, replica_groups=mesh['ctx'=8,'head'=4] {'ctx'}, dimensions={0}, use_global_device_ids=true | all-gather | bytes 589824 | tf_op jit(solution)/shard_map/all_gather | solution.py:173
  352.1 31.7 %all-gather.1 = bf16[16,128,128]{2,1,0:T(8,128)(2,1)S(1)} all-gather(bf16[2,128,128]{2,1,0:T(8,128)(2,1)S(1)} %convert_element_type.194), channel_id=3, replica_groups=mesh['ctx'=8,'head'=4] {'ctx'}, dimensions={0}, use_global_device_ids=true | all-gather | bytes 589824 | tf_op jit(solution)/shard_map/all_gather | solution.py:170
  393.8 4.1 all-to-all-start.5
  401.4 5.5 %all-to-all-done.5 = bf16[4,256,256]{2,1,0:T(8,128)(2,1)} async-done(((bf16[4,256,256]{2,1,0:T(8,128)(2,1)}), bf16[4,256,256]{2,1,0:T(8,128)(2,1)}, u32[]{:S(2)}, u32[]{:S(2)}) %all-to-all-start.5) | async-done | bytes 524320 | tf_op jit(solution)/shard_map/all_to_all | solution.py:204
  414.9 4.3 %all-to-all-done.6 = bf16[4,256,256]{2,1,0:T(8,128)(2,1)S(1)} async-done(((bf16[4,256,256]{2,1,0:T(8,128)(2,1)}), bf16[4,256,256]{2,1,0:T(8,128)(2,1)S(1)}, u32[]{:S(2)}, u32[]{:S(2)}) %all-to-all-start.6) | async-done | bytes 524320 | tf_op jit(solution)/shard_map/all_to_all | solution.py:205
  (322 shorter events, 159.9 us)
Async XLA Ops:
  7.2 6.2 %copy-start.63 = (f32[2,1024]{1,0:T(2,128)S(1)}, f32[2,1024]{1,0:T(2,128)}, u32[]{:S(2)}) copy-start(f32[2,1024]{1,0:T(2,128)} %param.10) | copy-start | bytes 24580
  7.2 7.9 %copy-start.54 = (bf16[256,1024]{1,0:T(8,128)(2,1)S(1)}, bf16[256,1024]{1,0:T(8,128)(2,1)}, u32[]{:S(2)}) copy-start(bf16[256,1024]{1,0:T(8,128)(2,1)} %param.8) | copy-start | bytes 1572868
  9.1 13.1 %all-to-all-start = ((bf16[256,4,256]{2,0,1:T(8,128)(2,1)}), bf16[256,4,256]{2,0,1:T(8,128)(2,1)S(1)}, u32[]{:S(2)}, u32[]{:S(2)}) async-start(bf16[256,4,256]{2,0,1:T(8,128)(2,1)} %bitcast.505), calls=%async_computation | async-start | bytes 1048576 | tf_op jit(solution)/shard_map/all_to_all | solution.py:106
  22.2 12.3 %all-to-all-start.1 = ((bf16[256,4,256]{2,0,1:T(8,128)(2,1)}), bf16[256,4,256]{2,0,1:T(8,128)(2,1)S(1)}, u32[]{:S(2)}, u32[]{:S(2)}) async-start(bf16[256,4,256]{2,0,1:T(8,128)(2,1)} %bitcast.504), calls=%async_computation.1 | async-start | bytes 1048576 | tf_op jit(solution)/shard_map/all_to_all | solution.py:107
  25.7 61.3 %all-gather.8.cloned.1.call-start = ((), (), s32[]{:S(2)}) async-start(), calls=%async_computation.8 | async-start | bytes 1179648 | tf_op jit(solution)/shard_map/all_gather | solution.py:144
  25.8 59.1 %copy-start.64 = (f32[2,2,512]{2,1,0:T(2,128)}, f32[2,2,512]{2,1,0:T(2,128)S(1)}, u32[]{:S(2)}) copy-start(f32[2,2,512]{2,1,0:T(2,128)S(1)} %reduce_window_sum.55) | copy-start | bytes 24580
  26.3 9.7 %copy-start.71 = (f32[2]{0:T(128)}, f32[2]{0:T(128)S(1)}, u32[]{:S(2)}) copy-start(f32[2]{0:T(128)S(1)} %get-tuple-element.20) | copy-start | bytes 28
  27.9 174.8 %copy-start.46 = (bf16[2,512,2,128]{1,3,0,2:T(8,128)(2,1)}, bf16[2,512,2,128]{1,3,0,2:T(8,128)(2,1)S(1)}, u32[]{:S(2)}) copy-start(bf16[2,512,2,128]{1,3,0,2:T(8,128)(2,1)S(1)} %copy.325) | copy-start | bytes 1572868
  34.6 38.4 %copy-start.48 = (bf16[2,512,2,128]{3,2,1,0:T(2,128)(2,1)}, bf16[2,512,2,128]{3,2,1,0:T(2,128)(2,1)S(1)}, u32[]{:S(2)}) copy-start(bf16[2,512,2,128]{3,2,1,0:T(2,128)(2,1)S(1)} %reshape.423) | copy-start | bytes 1572868
  36.0 30.4 %copy-start.56 = (bf16[256,1024]{1,0:T(8,128)(2,1)S(1)}, bf16[256,1024]{1,0:T(8,128)(2,1)}, u32[]{:S(2)}) copy-start(bf16[256,1024]{1,0:T(8,128)(2,1)} %param.6) | copy-start | bytes 1572868
  39.4 28.6 %all-to-all-start.2 = ((bf16[256,4,256]{2,0,1:T(8,128)(2,1)}), bf16[256,4,256]{2,0,1:T(8,128)(2,1)S(1)}, u32[]{:S(2)}, u32[]{:S(2)}) async-start(bf16[256,4,256]{2,0,1:T(8,128)(2,1)} %bitcast.503), calls=%async_computation.2 | async-start | bytes 1048576 | tf_op jit(solution)/shard_map/all_to_all | solution.py:108
  42.9 76.5 %all-gather.6.cloned.1.call-start = ((), (), s32[]{:S(2)}) async-start(), calls=%async_computation.7 | async-start | bytes 1179648 | tf_op jit(solution)/shard_map/all_gather | solution.py:145
  67.3 13.1 %copy-start.73 = (f32[2,2]{1,0:T(2,128)}, f32[2,2]{1,0:T(2,128)S(1)}, u32[]{:S(2)}) copy-start(f32[2,2]{1,0:T(2,128)S(1)} %pad_exponential_fusion) | copy-start | bytes 52
  68.0 12.3 %all-to-all-start.4 = ((bf16[256,4,256]{2,0,1:T(8,128)(2,1)}), bf16[256,4,256]{2,0,1:T(8,128)(2,1)S(1)}, u32[]{:S(2)}, u32[]{:S(2)}) async-start(bf16[256,4,256]{2,0,1:T(8,128)(2,1)} %bitcast.502), calls=%async_computation.4 | async-start | bytes 1048576 | tf_op jit(solution)/shard_map/all_to_all | solution.py:105
  74.1 7.3 %copy-start.57 = (pred[512,512]{1,0:T(8,128)(4,1)S(1)}, pred[512,512]{1,0:T(8,128)(4,1)}, u32[]{:S(2)}) copy-start(pred[512,512]{1,0:T(8,128)(4,1)} %iota_compare_fusion) | copy-start | bytes 786436
  74.2 48.8 %copy-start.42 = (bf16[2,512,2,128]{3,2,1,0:T(2,128)(2,1)}, bf16[2,512,2,128]{3,2,1,0:T(2,128)(2,1)S(1)}, u32[]{:S(2)}) copy-start(bf16[2,512,2,128]{3,2,1,0:T(2,128)(2,1)S(1)} %reshape.424) | copy-start | bytes 1572868
  292.0 9.8 %copy-start.35 = (f32[2,2,512,128]{2,3,1,0:T(8,128)S(1)}, f32[2,2,512,128]{2,3,1,0:T(8,128)}, u32[]{:S(2)}) copy-start(f32[2,2,512,128]{2,3,1,0:T(8,128)} %fusion.222) | copy-start | bytes 3145732
  292.0 9.8 %copy-start.36 = (f32[2,2,512,128]{2,3,1,0:T(8,128)S(1)}, f32[2,2,512,128]{2,3,1,0:T(8,128)}, u32[]{:S(2)}) copy-start(f32[2,2,512,128]{2,3,1,0:T(8,128)} %fusion.220) | copy-start | bytes 3145732
  296.8 5.0 %copy-start.33 = (f32[2,2,512,128]{2,3,1,0:T(8,128)S(1)}, f32[2,2,512,128]{2,3,1,0:T(8,128)}, u32[]{:S(2)}) copy-start(f32[2,2,512,128]{2,3,1,0:T(8,128)} %fusion.226) | copy-start | bytes 3145732
  296.9 5.0 %copy-start.34 = (f32[2,2,512,128]{2,3,1,0:T(8,128)S(1)}, f32[2,2,512,128]{2,3,1,0:T(8,128)}, u32[]{:S(2)}) copy-start(f32[2,2,512,128]{2,3,1,0:T(8,128)} %fusion.224) | copy-start | bytes 3145732
  296.9 5.0 %copy-start.69 = (f32[2,512,2]{1,0,2:T(2,128)S(1)}, f32[2,512,2]{1,0,2:T(2,128)}, u32[]{:S(2)}) copy-start(f32[2,512,2]{1,0,2:T(2,128)} %get-tuple-element.48) | copy-start | bytes 24580
  308.0 7.0 %copy-start.37 = (f32[2,2,512,128]{2,3,1,0:T(8,128)S(1)}, f32[2,2,512,128]{2,3,1,0:T(8,128)}, u32[]{:S(2)}) copy-start(f32[2,2,512,128]{2,3,1,0:T(8,128)} %multiply_add_fusion) | copy-start | bytes 3145732
  310.5 83.3 %all-to-all-start.3 = ((bf16[4,256,256]{2,1,0:T(8,128)(2,1)}), bf16[4,256,256]{2,1,0:T(8,128)(2,1)}, u32[]{:S(2)}, u32[]{:S(2)}) async-start(bf16[4,256,256]{2,1,0:T(8,128)(2,1)} %convert_element_type.176), calls=%async_computation.3 | async-start | bytes 1048576 | tf_op jit(solution)/shard_map/all_to_all | solution.py:203
  314.9 36.0 %copy-start.52 = (f32[2,2,128,128]{2,3,1,0:T(8,128)S(1)}, f32[2,2,128,128]{2,3,1,0:T(8,128)}, u32[]{:S(2)}) copy-start(f32[2,2,128,128]{2,3,1,0:T(8,128)} %convolution_bitcast_fusion.6) | copy-start | bytes 786436
  318.5 65.4 %copy-start.70 = (f32[2,8]{0,1:T(8,128)S(1)}, f32[2,8]{0,1:T(8,128)}, u32[]{:S(2)}) copy-start(f32[2,8]{0,1:T(8,128)} %select_bitcast_fusion) | copy-start | bytes 196
  319.6 64.7 %copy-start.72 = (f32[2]{0:T(128)S(1)}, f32[2]{0:T(128)}, u32[]{:S(2)}) copy-start(f32[2]{0:T(128)} %copy-done.71) | copy-start | bytes 28
  352.1 33.1 %copy-start.49 = (bf16[2,512,2,128]{3,2,1,0:T(2,128)(2,1)S(1)}, bf16[2,512,2,128]{3,2,1,0:T(2,128)(2,1)}, u32[]{:S(2)}) copy-start(bf16[2,512,2,128]{3,2,1,0:T(2,128)(2,1)} %copy-done.48) | copy-start | bytes 1572868
  352.1 33.1 %copy-start.50 = (f32[2,512,2,128]{3,1,0,2:T(8,128)S(1)}, f32[2,512,2,128]{3,1,0,2:T(8,128)}, u32[]{:S(2)}) copy-start(f32[2,512,2,128]{3,1,0,2:T(8,128)} %convolution_bitcast_fusion.2) | copy-start | bytes 3145732
  390.3 7.7 %copy-start.43 = (bf16[2,512,2,128]{3,2,1,0:T(2,128)(2,1)S(1)}, bf16[2,512,2,128]{3,2,1,0:T(2,128)(2,1)}, u32[]{:S(2)}) copy-start(bf16[2,512,2,128]{3,2,1,0:T(2,128)(2,1)} %copy-done.42) | copy-start | bytes 1572868
  390.3 7.7 %copy-start.44 = (bf16[2,2,512,512]{3,2,1,0:T(8,128)(2,1)S(1)}, bf16[2,2,512,512]{3,2,1,0:T(8,128)(2,1)}, u32[]{:S(2)}) copy-start(bf16[2,2,512,512]{3,2,1,0:T(8,128)(2,1)} %multiply_convert_fusion.1) | copy-start | bytes 6291460
  393.8 13.1 %all-to-all-start.5 = ((bf16[4,256,256]{2,1,0:T(8,128)(2,1)}), bf16[4,256,256]{2,1,0:T(8,128)(2,1)}, u32[]{:S(2)}, u32[]{:S(2)}) async-start(bf16[4,256,256]{2,1,0:T(8,128)(2,1)} %convert_element_type.202), calls=%async_computation.5 | async-start | bytes 1048576 | tf_op jit(solution)/shard_map/all_to_all | solution.py:204
  406.9 12.3 %all-to-all-start.6 = ((bf16[4,256,256]{2,1,0:T(8,128)(2,1)}), bf16[4,256,256]{2,1,0:T(8,128)(2,1)S(1)}, u32[]{:S(2)}, u32[]{:S(2)}) async-start(bf16[4,256,256]{2,1,0:T(8,128)(2,1)} %convert_element_type.204), calls=%async_computation.6 | async-start | bytes 1048576 | tf_op jit(solution)/shard_map/all_to_all | solution.py:205
  (53 other events, 127.9 us)
Sparse Core Ops, SparseCore 0:
  37.0 41.1 all-gather.7
  80.4 38.9 all-gather.5
where the time goes:
time: 433 us; the launch traced here: 428 us
  matrix products  144 us (33%)
  blocking collectives  85.4 us (20%)
  waiting for transfers between devices  61.2 us (14%)
  other arithmetic  52.5 us (12%)
  local copies, waits for them, and re-layouts  40.9 us (9%)
  starting transfers between devices  26.8 us (6%)
  between operations  16.7 us (4%)
    dot_general x23, matrix products, mixed(): return jnp.dot(left, right, preferred_element_type=jnp.float32)  90.3 us
    dot_general x20, matrix products, product(): jnp.dot(left.astype(jnp.float32), right.astype(jnp.float32), precision=hi...  45.7 us
    all_gather x1, waiting for transfers between devices, shards(): lax.all_gather(value_carry[None], 'ctx', axis=0, tiled=True)  32.4 us
    all_gather x1, blocking collectives, shards(): lax.all_gather(value_delta[None].astype(jnp.bfloat16), 'ctx', axis=0, til...  31.7 us
    all_gather x1, blocking collectives, shards(): lax.all_gather(gram_delta[None].astype(jnp.bfloat16), 'ctx', axis=0, tile...  31.3 us
    unnamed x1, blocking collectives  22.4 us
    reduce_sum x14, other arithmetic, conj_grad(): rho_next = jnp.sum(residual * residual, axis=-1, keepdims=True)  18.4 us
    unnamed x159, local copies, waits for them, and re-layouts  17.7 us
  transfers between devices with their start and end apart: 9, of which 6 were waited for; matrix products, arithmetic and copies ran while one was open for 10% of the time, Pallas kernels for 0%

commit v1 on v0

v1 whole, which is shorter than its diff:
```python
import functools

import jax
import jax.numpy as jnp
from jax import lax
from jax.experimental import pallas as pl
from jax.experimental.pallas import tpu as pltpu
from jax.sharding import PartitionSpec as P

DH = 128
SPAN = 512
SOLVE_STEPS = 8


highest = lax.Precision.HIGHEST
epsilon = 1e-06


CHUNK = 256
WORK_BYTES = 48 * 1024 * 1024


def dot(left, right, dims):
    return lax.dot_general(left, right, (dims, ((), ())), preferred_element_type=jnp.float32)


def dot_nn(left, right):
    return dot(left, right, ((1,), (0,)))


def dot_nt(left, right):
    return dot(left, right, ((1,), (1,)))


def dot_tn(left, right):
    return dot(left, right, ((0,), (0,)))


def low(array):
    return array.astype(jnp.bfloat16)


def two_parts(array):
    high = low(array)
    return high, low(array - high.astype(jnp.float32))


def running_sums(gate_row):
    size = gate_row.shape[1]
    rowpos = lax.broadcasted_iota(jnp.int32, (size, size), 0)
    column_position = lax.broadcasted_iota(jnp.int32, (size, size), 1)
    spread = jnp.broadcast_to(gate_row, (size, size))
    column = jnp.sum(jnp.where(rowpos >= column_position, spread, 0.0), axis=1, keepdims=True)
    gate_column = jnp.sum(jnp.where(rowpos == column_position, spread, 0.0), axis=1, keepdims=True)
    row = jnp.sum(jnp.where(rowpos <= column_position, gate_column, 0.0), axis=0, keepdims=True)
    return column, row, rowpos >= column_position


def solve_kernel(
    count, ridge_ref, gate_ref, q_ref, k_ref, v_ref, g_ref, gram_ref, value_ref,
    low_x_ref, low_y_ref, part_keys_ref, part_values_ref, value_back_ref, gram_back_ref,
    within_ref, decay_ref, stack_ref, x_ref, r_ref, p_ref, rho_ref,
):
    ridge = ridge_ref[pl.program_id(0) // count]
    column, row, causal = running_sums(gate_ref[0])
    within_ref[...] = jnp.where(causal, jnp.exp(jnp.minimum(column - row, 0.0)), 0.0)
    decay_ref[...] = jnp.broadcast_to(jnp.exp(column), decay_ref.shape)
    gram_high, gram_low = two_parts(gram_ref[0])
    stack_ref[0:DH] = gram_high
    stack_ref[DH : 2 * DH] = gram_high
    stack_ref[2 * DH : 3 * DH] = gram_low
    value_high, value_low = two_parts(value_ref[0])
    span = q_ref.shape[0]
    chunks = [(start, start + CHUNK) for start in range(0, span, CHUNK)]
    for start, stop in chunks:
        rows = slice(start, stop)
        grads = g_ref[rows]
        scores = low(within_ref[rows, 0:stop] * dot_nt(grads, v_ref[0:stop]))
        state = dot_nn(grads, value_high) + dot_nn(grads, value_low)
        rhs = decay_ref[rows] * state + dot_nn(scores, k_ref[0:stop])
        for side, first in enumerate((q_ref[rows].astype(jnp.float32), rhs)):
            x_ref[side, rows] = jnp.zeros_like(first)
            r_ref[side, rows] = first
            p_ref[side, rows] = first
            rho_ref[side, rows] = jnp.broadcast_to(
                jnp.sum(first * first, axis=1, keepdims=True), first.shape
            )

    def step(index, carry):
        for start, stop in chunks:
            rows = slice(start, stop)
            for side in range(2):
                direction = p_ref[side, rows]
                high, rest = two_parts(direction)
                scores = low(within_ref[rows, 0:stop] * dot_nt(high, k_ref[0:stop]))
                image = (
                    decay_ref[rows] * dot_nn(jnp.concatenate([high, rest, high], axis=1), stack_ref[...])
                    + dot_nn(scores, k_ref[0:stop])
                    + ridge * direction
                )
                rho_now = rho_ref[side, rows]
                curve = jnp.sum(direction * image, axis=1, keepdims=True)
                size = rho_now / (curve + epsilon)
                x_ref[side, rows] = x_ref[side, rows] + size * direction
                residual = r_ref[side, rows] - size * image
                r_ref[side, rows] = residual
                rho_next = jnp.sum(residual * residual, axis=1, keepdims=True)
                p_ref[side, rows] = residual + rho_next / (rho_now + epsilon) * direction
                rho_ref[side, rows] = jnp.broadcast_to(rho_next, residual.shape)
        return carry

    lax.fori_loop(0, SOLVE_STEPS, step, 0)
    solved = low(x_ref[0])
    adjoint = low(x_ref[1])
    low_x_ref[...] = solved
    low_y_ref[...] = adjoint
    weighted = low(decay_ref[...] * x_ref[0])
    value_back_ref[0] = dot_tn(g_ref[...], weighted)
    gram_back_ref[0] = -dot_tn(adjoint, weighted)
    for start, stop in chunks:
        rows = slice(start, stop)
        within = within_ref[start:, rows]
        solved_now, adjoint_now, grads = low_x_ref[start:], low_y_ref[start:], g_ref[start:]
        along_solved = low(within * dot_nt(solved_now, k_ref[rows]))
        along_adjoint = low(within * dot_nt(adjoint_now, k_ref[rows]))
        along_values = low(within * dot_nt(grads, v_ref[rows]))
        part_values_ref[rows] = dot_tn(along_solved, grads)
        part_keys_ref[rows] = (
            dot_tn(along_values, solved_now)
            - dot_tn(along_solved, adjoint_now)
            - dot_tn(along_adjoint, solved_now)
        )


def solve_blocks(ridge, log_decay, queries, keys, values, grads_out, gram_start, value_start):
    rows, width = queries.shape
    head_dev = width // DH
    count = rows // SPAN
    units = head_dev * count
    gates = log_decay.reshape(units, 1, SPAN)
    part = pl.BlockSpec((SPAN, DH), lambda u: (u % count, u // count))
    state = pl.BlockSpec((1, DH, DH), lambda u: (u, 0, 0))
    low_shape = jax.ShapeDtypeStruct((rows, width), jnp.bfloat16)
    wide_shape = jax.ShapeDtypeStruct((rows, width), jnp.float32)
    state_shape = jax.ShapeDtypeStruct((units, DH, DH), jnp.float32)
    work = pltpu.VMEM((2, SPAN, DH), jnp.float32)
    return pl.pallas_call(
        functools.partial(solve_kernel, count),
        grid=(units,),
        out_shape=(low_shape, low_shape, wide_shape, wide_shape, state_shape, state_shape),
        in_specs=[
            pl.BlockSpec(memory_space=pltpu.SMEM),
            pl.BlockSpec((1, 1, SPAN), lambda u: (u, 0, 0)),
            part, part, part, part, state, state,
        ],
        out_specs=(part, part, part, part, state, state),
        scratch_shapes=[
            pltpu.VMEM((SPAN, SPAN), jnp.float32),
            pltpu.VMEM((SPAN, DH), jnp.float32),
            pltpu.VMEM((3 * DH, DH), jnp.bfloat16),
            work, work, work, work,
        ],
        compiler_params=pltpu.CompilerParams(vmem_limit_bytes=WORK_BYTES),
        name="solve_blocks",
    )(ridge, gates, queries, keys, values, grads_out, gram_start, value_start)


def split_heads(block, head_dev):
    rows = block.shape[0]
    return block.reshape(rows // SPAN, SPAN, head_dev, DH).transpose(2, 0, 1, 3)


def wide_heads(block):
    head_dev, count, size, width = block.shape
    return block.transpose(1, 2, 0, 3).reshape(count * size, head_dev * width)


def scale_mats(factor, mats):
    return factor[..., None, None] * mats


def shards(queries, keys, values, grads_out, log_decay, ridge):
    gathered = (
        lax.all_to_all(queries, "head", split_axis=1, concat_axis=0, tiled=True),
        lax.all_to_all(keys, "head", split_axis=1, concat_axis=0, tiled=True),
        lax.all_to_all(values, "head", split_axis=1, concat_axis=0, tiled=True),
        lax.all_to_all(grads_out, "head", split_axis=1, concat_axis=0, tiled=True),
    )
    head_dev = log_decay.shape[0]
    query_h = split_heads(gathered[0], head_dev)
    key_h = split_heads(gathered[1], head_dev)
    value_h = split_heads(gathered[2], head_dev)
    grad_h = split_heads(gathered[3], head_dev)
    count = query_h.shape[1]
    gates = log_decay.reshape(head_dev, count, SPAN)
    sums = jnp.sum(gates, axis=2)
    through_local = jnp.cumsum(sums, axis=1)
    starts = jnp.concatenate([jnp.zeros_like(sums[:, :1]), through_local[:, :-1]], axis=1)
    total_log = jnp.sum(sums, axis=1)
    cumul = jnp.cumsum(gates, axis=2)
    key_wide = key_h.astype(jnp.float32)
    scaled_lookup_vectors = jnp.exp(cumul[..., -1:] - cumul)[..., None] * key_wide
    gram_parts = jnp.einsum("hnck,hncl->hnkl", key_wide, scaled_lookup_vectors, precision=highest)
    value_parts = jnp.einsum(
        "hncv,hnck->hnvk", value_h.astype(jnp.float32), scaled_lookup_vectors, precision=highest
    )
    zeros = jnp.zeros((head_dev, DH, DH), jnp.float32)
    gram_carry, value_carry = (zeros, zeros)
    gram_local, value_local = ([], [])
    for block in range(count):
        gram_local.append(gram_carry)
        value_local.append(value_carry)
        decay = jnp.exp(sums[:, block])
        gram_carry = scale_mats(decay, gram_carry) + gram_parts[:, block]
        value_carry = scale_mats(decay, value_carry) + value_parts[:, block]
    position = lax.axis_index("ctx")
    totals = lax.all_gather(total_log[None], "ctx", axis=0, tiled=True)
    through = jnp.cumsum(totals, axis=0)
    exclusive = jnp.concatenate([jnp.zeros_like(totals[:1]), through[:-1]], axis=0)
    mine_excl = lax.dynamic_slice_in_dim(exclusive, position, 1, 0)
    mine_through = lax.dynamic_slice_in_dim(through, position, 1, 0)
    piece = (
        lax.all_gather(gram_carry[None], "ctx", axis=0, tiled=True),
        lax.all_gather(value_carry[None], "ctx", axis=0, tiled=True),
    )
    number = piece[0].shape[0]
    index = jnp.arange(number, dtype=jnp.int32)
    gap = mine_excl - through
    weight = jnp.where((index < position)[:, None], jnp.exp(jnp.minimum(gap, 0.0)), 0.0)
    gram_in = jnp.einsum("jh,jhkl->hkl", weight, piece[0], precision=highest)
    value_in = jnp.einsum("jh,jhkl->hkl", weight, piece[1], precision=highest)
    entry = jnp.exp(starts)
    gram_start = scale_mats(entry, gram_in[:, None]) + jnp.stack(gram_local, axis=1)
    value_start = scale_mats(entry, value_in[:, None]) + jnp.stack(value_local, axis=1)
    units = head_dev * count
    solved, adjoint, part_keys, part_values, value_back, gram_back = solve_blocks(
        ridge,
        log_decay,
        *gathered,
        gram_start.reshape(units, DH, DH),
        value_start.reshape(units, DH, DH),
    )
    value_back = value_back.reshape(head_dev, count, DH, DH)
    gram_back = gram_back.reshape(head_dev, count, DH, DH)
    value_delta = jnp.einsum("hn,hnvk->hvk", entry, value_back, precision=highest)
    gram_delta = jnp.einsum("hn,hnvk->hvk", entry, gram_back, precision=highest)
    piece = (
        lax.all_gather(value_delta[None].astype(jnp.bfloat16), "ctx", axis=0, tiled=True).astype(
            jnp.float32
        ),
        lax.all_gather(gram_delta[None].astype(jnp.bfloat16), "ctx", axis=0, tiled=True).astype(
            jnp.float32
        ),
    )
    number = piece[0].shape[0]
    index = jnp.arange(number, dtype=jnp.int32)
    gap = exclusive - mine_through
    weight = jnp.where((index > position)[:, None], jnp.exp(jnp.minimum(gap, 0.0)), 0.0)
    value_after = zeros + jnp.einsum("jh,jhkl->hkl", weight, piece[0], precision=highest)
    outer_product_suffix = zeros + jnp.einsum("jh,jhkl->hkl", weight, piece[1], precision=highest)
    value_next = [None] * count
    gram_next = [None] * count
    for block in reversed(range(count)):
        value_next[block] = value_after
        gram_next[block] = outer_product_suffix
        decay = jnp.exp(sums[:, block])
        value_after = scale_mats(decay, value_after) + value_back[:, block]
        outer_product_suffix = scale_mats(decay, outer_product_suffix) + gram_back[:, block]
    end_weight = jnp.exp(cumul[..., -1:] - cumul)[..., None]
    value_next = jnp.stack(value_next, axis=1)
    gram_next = jnp.stack(gram_next, axis=1)
    gram_next = low(gram_next + gram_next.swapaxes(2, 3))
    value_next = low(value_next)
    add_values = end_weight * jnp.einsum(
        "hnck,hnvk->hncv", key_h, value_next, preferred_element_type=jnp.float32
    )
    add_keys = end_weight * (
        jnp.einsum("hncv,hnvk->hnck", value_h, value_next, preferred_element_type=jnp.float32)
        + jnp.einsum("hnck,hnkl->hncl", key_h, gram_next, preferred_element_type=jnp.float32)
    )
    grad_keys = low(part_keys + wide_heads(add_keys))
    grad_values = low(part_values + wide_heads(add_values))
    results = (
        lax.all_to_all(adjoint, "head", split_axis=0, concat_axis=1, tiled=True),
        lax.all_to_all(grad_keys, "head", split_axis=0, concat_axis=1, tiled=True),
        lax.all_to_all(grad_values, "head", split_axis=0, concat_axis=1, tiled=True),
    )
    return (results[0], results[1], results[2])


def solution(mesh):
    return jax.shard_map(
        shards,
        mesh=mesh,
        in_specs=(
            P(("ctx", "head"), None),
            P(("ctx", "head"), None),
            P(("ctx", "head"), None),
            P(("ctx", "head"), None),
            P("head", "ctx"),
            P("head"),
        ),
        out_specs=(P(("ctx", "head"), None), P(("ctx", "head"), None), P(("ctx", "head"), None)),
        check_vma=False,
    )
```

time: 433 us -> 279 us (0.64)
  matrix products: 144 us -> 5.76 us
  Pallas kernels: 0 us -> 41.9 us
  other arithmetic: 52.5 us -> 10.8 us
  local copies, waits for them, and re-layouts: 40.9 us -> 20 us
  waiting for transfers between devices: 61.2 us -> 73.2 us
    dot_general x45 -> x3, matrix products: 141 us -> 0.96 us  [the longest x1 0.35 us: shards(): jnp.einsum('hnck,hnvk->hncv', key_h, value_next, preferred_element_type=j...]
    pallas_call x0 -> x1, Pallas kernels: none -> 41.9 us  [solve_blocks(): pl.pallas_call(functools.partial(solve_kernel, count), grid=(units,), out...]
    reduce_sum x14 -> x0, other arithmetic: 18.4 us -> none  [conj_grad(): rho_next = jnp.sum(residual * residual, axis=-1, keepdims=True)]
    add x15 -> x1, other arithmetic: 15.7 us -> 1.01 us  [shards(): scale_mats(entry, value_in[:, None]) + jnp.stack(value_local, axis=1)]
    unnamed x159 -> x40, local copies, waits for them, and re-layouts: 17.7 us -> 6.11 us
    all_gather x1, waiting for transfers between devices: 32.4 us -> 41.1 us  [shards(): lax.all_gather(value_carry[None], 'ctx', axis=0, tiled=True)]
    convert_element_type x6 -> x0, local copies, waits for them, and re-layouts: 7.7 us -> none  [join_heads(): block.transpose(1, 2, 0, 3).reshape(count * size, head_dev * width)]
    all_to_all x1, waiting for transfers between devices: 6.03 us -> 0.01 us  [shards(): lax.all_to_all(queries, 'head', split_axis=1, concat_axis=0, tiled=True)]
  transfers between devices with their start and end apart: 9 -> 9, of which waited for: 6 -> 6; matrix products, arithmetic and copies ran while one was open for 10% -> 8% of each run, Pallas kernels for 0% -> 0%
where the time goes in v1:
time: 279 us; the launch traced here: 278 us
  blocking collectives  85.6 us (31%)
  waiting for transfers between devices  73.2 us (26%)
  Pallas kernels  41.9 us (15%)
  starting transfers between devices  25.4 us (9%)
  local copies, waits for them, and re-layouts  20 us (7%)
  between operations  15.1 us (5%)
  other arithmetic  10.8 us (4%)
  matrix products  5.76 us (2%)
    pallas_call x1, Pallas kernels, solve_blocks(): pl.pallas_call(functools.partial(solve_kernel, count), grid=(units,), out...  41.9 us
    all_gather x1, waiting for transfers between devices, shards(): lax.all_gather(value_carry[None], 'ctx', axis=0, tiled=True)  41.1 us
    all_gather x1, blocking collectives, shards(): lax.all_gather(value_delta[None].astype(jnp.bfloat16), 'ctx', axis=0, til...  31.9 us
    all_gather x1, blocking collectives, shards(): lax.all_gather(gram_delta[None].astype(jnp.bfloat16), 'ctx', axis=0, tile...  31.3 us
    unnamed x1, blocking collectives  22.4 us
    all_to_all x1, waiting for transfers between devices, shards(): lax.all_to_all(values, 'head', split_axis=1, concat_axis=0, tiled=True)  7.97 us
    all_to_all x1, waiting for transfers between devices, shards(): lax.all_to_all(grad_values, 'head', split_axis=0, concat_axis=1, tiled=True)  7.09 us
    all_to_all x1, waiting for transfers between devices, shards(): lax.all_to_all(keys, 'head', split_axis=1, concat_axis=0, tiled=True)  6.26 us
  transfers between devices with their start and end apart: 9, of which 6 were waited for; matrix products, arithmetic and copies ran while one was open for 8% of the time, Pallas kernels for 0%

profile of v1, /device:TPU:0, one launch (start us, length us, event | category | flops | bytes accessed | tf_op | source)
XLA Modules:
  0.0 277.8 jit_solution(15000813649861390137)
XLA Ops:
  7.2 1.9 copy.205
  9.0 4.4 %all-to-all-start.1 = ((bf16[256,4,256]{2,0,1:T(8,128)(2,1)}), bf16[256,4,256]{2,0,1:T(8,128)(2,1)S(1)}, u32[]{:S(2)}, u32[]{:S(2)}) async-start(bf16[256,4,256]{2,0,1:T(8,128)(2,1)} %bitcast.164), calls=%async_computation.1 | async-start | bytes 1048576 | tf_op jit(solution)/shard_map/all_to_all | solution.py:185
  13.4 1.2 reduce-window.6
  16.0 6.3 %all-to-all-done.1 = bf16[256,4,256]{2,0,1:T(8,128)(2,1)S(1)} async-done(((bf16[256,4,256]{2,0,1:T(8,128)(2,1)}), bf16[256,4,256]{2,0,1:T(8,128)(2,1)S(1)}, u32[]{:S(2)}, u32[]{:S(2)}) %all-to-all-start.1) | async-done | bytes 524320 | tf_op jit(solution)/shard_map/all_to_all | solution.py:185
  22.3 3.5 %all-to-all-start.2 = ((bf16[256,4,256]{2,0,1:T(8,128)(2,1)}), bf16[256,4,256]{2,0,1:T(8,128)(2,1)S(1)}, u32[]{:S(2)}, u32[]{:S(2)}) async-start(bf16[256,4,256]{2,0,1:T(8,128)(2,1)} %bitcast.163), calls=%async_computation.2 | async-start | bytes 1048576 | tf_op jit(solution)/shard_map/all_to_all | solution.py:186
  26.6 8.0 %all-to-all-done.2 = bf16[256,4,256]{2,0,1:T(8,128)(2,1)S(1)} async-done(((bf16[256,4,256]{2,0,1:T(8,128)(2,1)}), bf16[256,4,256]{2,0,1:T(8,128)(2,1)S(1)}, u32[]{:S(2)}, u32[]{:S(2)}) %all-to-all-start.2) | async-done | bytes 524320 | tf_op jit(solution)/shard_map/all_to_all | solution.py:186
  34.7 1.3 convolution_bitcast_fusion.2
  36.0 1.3 convolution_bitcast_fusion.1
  42.2 3.6 %all-to-all-start = ((bf16[256,4,256]{2,0,1:T(8,128)(2,1)}), bf16[256,4,256]{2,0,1:T(8,128)(2,1)S(1)}, u32[]{:S(2)}, u32[]{:S(2)}) async-start(bf16[256,4,256]{2,0,1:T(8,128)(2,1)} %bitcast.165), calls=%async_computation | async-start | bytes 1048576 | tf_op jit(solution)/shard_map/all_to_all | solution.py:184
  45.8 22.4 %all-reduce.4 = f32[16]{0:T(128)S(1)} all-reduce(f32[16]{0:T(128)S(1)} %dynamic-update-slice), channel_id=2, replica_groups=mesh['ctx'=8,'head'=4] {'ctx'}, use_global_device_ids=true, to_apply=%add.4 | all-reduce | flops 16 | bytes 128
  71.1 3.5 %all-to-all-start.3 = ((bf16[256,4,256]{2,0,1:T(8,128)(2,1)}), bf16[256,4,256]{2,0,1:T(8,128)(2,1)S(1)}, u32[]{:S(2)}, u32[]{:S(2)}) async-start(bf16[256,4,256]{2,0,1:T(8,128)(2,1)} %bitcast.162), calls=%async_computation.3 | async-start | bytes 1048576 | tf_op jit(solution)/shard_map/all_to_all | solution.py:187
  74.6 5.0 %all-gather.6.cloned.1.call-done = f32[8,2,128,128]{3,2,1,0:T(8,128)} async-done(((f32[1,2,128,128]{3,2,1,0:T(8,128)}), f32[8,2,128,128]{3,2,1,0:T(8,128)}) %all-gather.6.cloned.1.call-update) | async-done | bytes 1048592 | tf_op jit(solution)/shard_map/all_gather | solution.py:223
  79.6 41.1 %all-gather.8.cloned.1.call-done = f32[8,2,128,128]{3,2,1,0:T(8,128)} async-done(((f32[1,2,128,128]{3,2,1,0:T(8,128)}), f32[8,2,128,128]{3,2,1,0:T(8,128)}) %all-gather.8.cloned.1.call-update) | async-done | bytes 1048592 | tf_op jit(solution)/shard_map/all_gather | solution.py:224
  120.7 1.8 multiply_reduce_fusion.2
  124.0 1.0 pad_add_fusion
  126.0 41.9 %solve_blocks.1 = (bf16[1024,256]{1,0:T(8,128)(2,1)}, bf16[1024,256]{1,0:T(8,128)(2,1)}, f32[1024,256]{1,0:T(8,128)S(1)}, f32[1024,256]{1,0:T(8,128)}, f32[4,128...) custom-call(f32[2]{0:T(128)S(1)} %copy-done.2, f32[4,1,512]{2,1,0:T(1,128)S(1)} %reshape.154.gate_ref, ...), custom_call_target="tpu_custom_call" | custom-call | tf_op jit(solution)/shard_map/solve_blocks/pallas_call | solution.py:147
  167.9 1.0 copy-done
  169.6 1.1 fusion.20
  170.7 1.1 fusion.18
  171.8 3.5 %all-to-all-start.4 = ((bf16[4,256,256]{2,1,0:T(8,128)(2,1)}), bf16[4,256,256]{2,1,0:T(8,128)(2,1)S(1)}, u32[]{:S(2)}, u32[]{:S(2)}) async-start(bf16[4,256,256]{2,1,0:T(8,128)(2,1)} %bitcast.30), calls=%async_computation.4 | async-start | bytes 1048576 | tf_op jit(solution)/shard_map/all_to_all | solution.py:284
  175.5 31.3 %all-gather.2 = bf16[16,128,128]{2,1,0:T(8,128)(2,1)S(1)} all-gather(bf16[2,128,128]{2,1,0:T(8,128)(2,1)S(1)} %convert_element_type.31), channel_id=4, replica_groups=mesh['ctx'=8,'head'=4] {'ctx'}, dimensions={0}, use_global_device_ids=true | all-gather | bytes 589824 | tf_op jit(solution)/shard_map/all_gather | solution.py:251
  206.8 31.9 %all-gather.1 = bf16[16,128,128]{2,1,0:T(8,128)(2,1)S(1)} all-gather(bf16[2,128,128]{2,1,0:T(8,128)(2,1)S(1)} %convert_element_type.29), channel_id=3, replica_groups=mesh['ctx'=8,'head'=4] {'ctx'}, dimensions={0}, use_global_device_ids=true | all-gather | bytes 589824 | tf_op jit(solution)/shard_map/all_gather | solution.py:248
  242.1 1.3 copy.104
  243.4 2.1 fusion.4
  245.5 3.5 %all-to-all-start.5 = ((bf16[4,256,256]{2,1,0:T(8,128)(2,1)}), bf16[4,256,256]{2,1,0:T(8,128)(2,1)S(1)}, u32[]{:S(2)}, u32[]{:S(2)}) async-start(bf16[4,256,256]{2,1,0:T(8,128)(2,1)} %bitcast.56), calls=%async_computation.5 | async-start | bytes 1048576 | tf_op jit(solution)/shard_map/all_to_all | solution.py:285
  249.9 2.1 fusion.3
  252.1 5.7 %all-to-all-done.5 = bf16[4,256,256]{2,1,0:T(8,128)(2,1)S(1)} async-done(((bf16[4,256,256]{2,1,0:T(8,128)(2,1)}), bf16[4,256,256]{2,1,0:T(8,128)(2,1)S(1)}, u32[]{:S(2)}, u32[]{:S(2)}) %all-to-all-start.5) | async-done | bytes 524320 | tf_op jit(solution)/shard_map/all_to_all | solution.py:285
  257.8 3.5 %all-to-all-start.6 = ((bf16[4,256,256]{2,1,0:T(8,128)(2,1)}), bf16[4,256,256]{2,1,0:T(8,128)(2,1)S(1)}, u32[]{:S(2)}, u32[]{:S(2)}) async-start(bf16[4,256,256]{2,1,0:T(8,128)(2,1)} %bitcast.59), calls=%async_computation.6 | async-start | bytes 1048576 | tf_op jit(solution)/shard_map/all_to_all | solution.py:286
  261.3 0.9 copy.159
  262.1 0.9 copy.160
  263.0 7.1 %all-to-all-done.6 = bf16[4,256,256]{2,1,0:T(8,128)(2,1)S(1)} async-done(((bf16[4,256,256]{2,1,0:T(8,128)(2,1)}), bf16[4,256,256]{2,1,0:T(8,128)(2,1)S(1)}, u32[]{:S(2)}, u32[]{:S(2)}) %all-to-all-start.6) | async-done | bytes 524320 | tf_op jit(solution)/shard_map/all_to_all | solution.py:286
  270.1 0.9 copy.161
  (97 shorter events, 16.8 us)
Async XLA Ops:
  9.0 4.4 %copy-start.9 = (f32[2,1024]{1,0:T(2,128)S(1)}, f32[2,1024]{1,0:T(2,128)}, u32[]{:S(2)}) copy-start(f32[2,1024]{1,0:T(2,128)} %param.10) | copy-start | bytes 24580
  9.0 6.1 %copy-start.6 = (bf16[256,1024]{1,0:T(8,128)(2,1)S(1)}, bf16[256,1024]{1,0:T(8,128)(2,1)}, u32[]{:S(2)}) copy-start(bf16[256,1024]{1,0:T(8,128)(2,1)} %param.8) | copy-start | bytes 1572868
  9.0 13.2 %all-to-all-start.1 = ((bf16[256,4,256]{2,0,1:T(8,128)(2,1)}), bf16[256,4,256]{2,0,1:T(8,128)(2,1)S(1)}, u32[]{:S(2)}, u32[]{:S(2)}) async-start(bf16[256,4,256]{2,0,1:T(8,128)(2,1)} %bitcast.164), calls=%async_computation.1 | async-start | bytes 1048576 | tf_op jit(solution)/shard_map/all_to_all | solution.py:185
  22.3 12.3 %all-to-all-start.2 = ((bf16[256,4,256]{2,0,1:T(8,128)(2,1)}), bf16[256,4,256]{2,0,1:T(8,128)(2,1)S(1)}, u32[]{:S(2)}, u32[]{:S(2)}) async-start(bf16[256,4,256]{2,0,1:T(8,128)(2,1)} %bitcast.163), calls=%async_computation.2 | async-start | bytes 1048576 | tf_op jit(solution)/shard_map/all_to_all | solution.py:186
  25.7 53.9 %all-gather.6.cloned.1.call-start = ((), (), s32[]{:S(2)}) async-start(), calls=%async_computation.7 | async-start | bytes 1179648 | tf_op jit(solution)/shard_map/all_gather | solution.py:223
  26.3 11.0 %copy-start.11 = (f32[2]{0:T(128)}, f32[2]{0:T(128)S(1)}, u32[]{:S(2)}) copy-start(f32[2]{0:T(128)S(1)} %get-tuple-element.17) | copy-start | bytes 28
  34.7 1.4 copy-start.3
  37.5 1.7 copy-start.7
  38.3 82.4 %all-gather.8.cloned.1.call-start = ((), (), s32[]{:S(2)}) async-start(), calls=%async_computation.8 | async-start | bytes 1179648 | tf_op jit(solution)/shard_map/all_gather | solution.py:224
  40.1 0.7 copy-start.16
  42.2 27.1 %copy-start.8 = (bf16[256,1024]{1,0:T(8,128)(2,1)S(1)}, bf16[256,1024]{1,0:T(8,128)(2,1)}, u32[]{:S(2)}) copy-start(bf16[256,1024]{1,0:T(8,128)(2,1)} %param.9) | copy-start | bytes 1572868
  42.2 28.9 %all-to-all-start = ((bf16[256,4,256]{2,0,1:T(8,128)(2,1)}), bf16[256,4,256]{2,0,1:T(8,128)(2,1)S(1)}, u32[]{:S(2)}, u32[]{:S(2)}) async-start(bf16[256,4,256]{2,0,1:T(8,128)(2,1)} %bitcast.165), calls=%async_computation | async-start | bytes 1048576 | tf_op jit(solution)/shard_map/all_to_all | solution.py:184
  68.6 0.7 copy-start.14
  71.1 54.2 %all-to-all-start.3 = ((bf16[256,4,256]{2,0,1:T(8,128)(2,1)}), bf16[256,4,256]{2,0,1:T(8,128)(2,1)S(1)}, u32[]{:S(2)}, u32[]{:S(2)}) async-start(bf16[256,4,256]{2,0,1:T(8,128)(2,1)} %bitcast.162), calls=%async_computation.3 | async-start | bytes 1048576 | tf_op jit(solution)/shard_map/all_to_all | solution.py:187
  123.3 0.7 copy-start.13
  125.3 0.7 copy-start.2
  167.9 1.0 copy-start
  168.9 0.7 copy-start.15
  171.8 73.7 %all-to-all-start.4 = ((bf16[4,256,256]{2,1,0:T(8,128)(2,1)}), bf16[4,256,256]{2,1,0:T(8,128)(2,1)S(1)}, u32[]{:S(2)}, u32[]{:S(2)}) async-start(bf16[4,256,256]{2,1,0:T(8,128)(2,1)} %bitcast.30), calls=%async_computation.4 | async-start | bytes 1048576 | tf_op jit(solution)/shard_map/all_to_all | solution.py:284
  206.8 31.9 %copy-start.10 = (f32[2,8]{0,1:T(8,128)S(1)}, f32[2,8]{0,1:T(8,128)}, u32[]{:S(2)}) copy-start(f32[2,8]{0,1:T(8,128)} %select_bitcast_fusion) | copy-start | bytes 196
  239.0 0.6 copy-start.12
  239.8 1.0 copy-start.4
  240.8 0.9 copy-start.5
  242.1 1.3 copy-start.1
  245.5 12.3 %all-to-all-start.5 = ((bf16[4,256,256]{2,1,0:T(8,128)(2,1)}), bf16[4,256,256]{2,1,0:T(8,128)(2,1)S(1)}, u32[]{:S(2)}, u32[]{:S(2)}) async-start(bf16[4,256,256]{2,1,0:T(8,128)(2,1)} %bitcast.56), calls=%async_computation.5 | async-start | bytes 1048576 | tf_op jit(solution)/shard_map/all_to_all | solution.py:285
  257.8 12.3 %all-to-all-start.6 = ((bf16[4,256,256]{2,1,0:T(8,128)(2,1)}), bf16[4,256,256]{2,1,0:T(8,128)(2,1)S(1)}, u32[]{:S(2)}, u32[]{:S(2)}) async-start(bf16[4,256,256]{2,1,0:T(8,128)(2,1)} %bitcast.59), calls=%async_computation.6 | async-start | bytes 1048576 | tf_op jit(solution)/shard_map/all_to_all | solution.py:286
Sparse Core Ops, SparseCore 0:
  38.4 41.1 all-gather.5
  81.7 38.8 all-gather.7

commit v2 on v1

v2 whole, which is shorter than its diff:
```python
import functools

import jax
import jax.numpy as jnp
from jax import lax
from jax.experimental import pallas as pl
from jax.experimental.pallas import tpu as pltpu
from jax.sharding import PartitionSpec as P

DH = 128
SPAN = 512
SOLVE_STEPS = 8


epsilon = 1e-06


CHUNK = 256
WORK_BYTES = 48 * 1024 * 1024


def dot(left, right, dims):
    return lax.dot_general(left, right, (dims, ((), ())), preferred_element_type=jnp.float32)


def dot_nn(left, right):
    return dot(left, right, ((1,), (0,)))


def dot_nt(left, right):
    return dot(left, right, ((1,), (1,)))


def dot_tn(left, right):
    return dot(left, right, ((0,), (0,)))


def low(array):
    return array.astype(jnp.bfloat16)


def two_parts(array):
    high = low(array)
    return high, low(array - high.astype(jnp.float32))


def running_sums(gate_row):
    size = gate_row.shape[1]
    rowpos = lax.broadcasted_iota(jnp.int32, (size, size), 0)
    column_position = lax.broadcasted_iota(jnp.int32, (size, size), 1)
    spread = jnp.broadcast_to(gate_row, (size, size))
    column = jnp.sum(jnp.where(rowpos >= column_position, spread, 0.0), axis=1, keepdims=True)
    gate_column = jnp.sum(jnp.where(rowpos == column_position, spread, 0.0), axis=1, keepdims=True)
    row = jnp.sum(jnp.where(rowpos <= column_position, gate_column, 0.0), axis=0, keepdims=True)
    return column, row, rowpos >= column_position


def solve_kernel(
    count, ridge_ref, gate_ref, q_ref, k_ref, v_ref, g_ref, gram_ref, value_ref,
    low_x_ref, low_y_ref, part_keys_ref, part_values_ref, value_back_ref, gram_back_ref,
    within_ref, decay_ref, stack_ref, x_ref, r_ref, p_ref, rho_ref,
):
    ridge = ridge_ref[pl.program_id(0) // count]
    column, row, causal = running_sums(gate_ref[0])
    within_ref[...] = jnp.where(causal, jnp.exp(jnp.minimum(column - row, 0.0)), 0.0)
    decay_ref[...] = jnp.broadcast_to(jnp.exp(column), decay_ref.shape)
    gram_high, gram_low = two_parts(gram_ref[0])
    stack_ref[0:DH] = gram_high
    stack_ref[DH : 2 * DH] = gram_high
    stack_ref[2 * DH : 3 * DH] = gram_low
    value_high, value_low = two_parts(value_ref[0])
    span = q_ref.shape[0]
    chunks = [(start, start + CHUNK) for start in range(0, span, CHUNK)]
    for start, stop in chunks:
        rows = slice(start, stop)
        grads = g_ref[rows]
        scores = low(within_ref[rows, 0:stop] * dot_nt(grads, v_ref[0:stop]))
        state = dot_nn(grads, value_high) + dot_nn(grads, value_low)
        rhs = decay_ref[rows] * state + dot_nn(scores, k_ref[0:stop])
        for side, first in enumerate((q_ref[rows].astype(jnp.float32), rhs)):
            x_ref[side, rows] = jnp.zeros_like(first)
            r_ref[side, rows] = first
            p_ref[side, rows] = first
            rho_ref[side, rows] = jnp.broadcast_to(
                jnp.sum(first * first, axis=1, keepdims=True), first.shape
            )

    def step(index, carry):
        for start, stop in chunks:
            rows = slice(start, stop)
            for side in range(2):
                direction = p_ref[side, rows]
                high, rest = two_parts(direction)
                scores = low(within_ref[rows, 0:stop] * dot_nt(high, k_ref[0:stop]))
                image = (
                    decay_ref[rows] * dot_nn(jnp.concatenate([high, rest, high], axis=1), stack_ref[...])
                    + dot_nn(scores, k_ref[0:stop])
                    + ridge * direction
                )
                rho_now = rho_ref[side, rows]
                curve = jnp.sum(direction * image, axis=1, keepdims=True)
                size = rho_now / (curve + epsilon)
                x_ref[side, rows] = x_ref[side, rows] + size * direction
                residual = r_ref[side, rows] - size * image
                r_ref[side, rows] = residual
                rho_next = jnp.sum(residual * residual, axis=1, keepdims=True)
                p_ref[side, rows] = residual + rho_next / (rho_now + epsilon) * direction
                rho_ref[side, rows] = jnp.broadcast_to(rho_next, residual.shape)
        return carry

    lax.fori_loop(0, SOLVE_STEPS, step, 0)
    solved = low(x_ref[0])
    adjoint = low(x_ref[1])
    low_x_ref[...] = solved
    low_y_ref[...] = adjoint
    weighted = low(decay_ref[...] * x_ref[0])
    value_back_ref[0] = dot_tn(g_ref[...], weighted)
    gram_back_ref[0] = -dot_tn(adjoint, weighted)
    for start, stop in chunks:
        rows = slice(start, stop)
        within = within_ref[start:, rows]
        solved_now, adjoint_now, grads = low_x_ref[start:], low_y_ref[start:], g_ref[start:]
        along_solved = low(within * dot_nt(solved_now, k_ref[rows]))
        along_adjoint = low(within * dot_nt(adjoint_now, k_ref[rows]))
        along_values = low(within * dot_nt(grads, v_ref[rows]))
        part_values_ref[rows] = dot_tn(along_solved, grads)
        part_keys_ref[rows] = (
            dot_tn(along_values, solved_now)
            - dot_tn(along_solved, adjoint_now)
            - dot_tn(along_adjoint, solved_now)
        )


def solve_blocks(ridge, gates, queries, keys, values, grads_out, gram_start, value_start):
    rows, width = queries.shape
    head_dev = width // DH
    count = rows // SPAN
    units = head_dev * count
    part = pl.BlockSpec((SPAN, DH), lambda u: (u % count, u // count))
    state = pl.BlockSpec((1, DH, DH), lambda u: (u, 0, 0))
    low_shape = jax.ShapeDtypeStruct((rows, width), jnp.bfloat16)
    wide_shape = jax.ShapeDtypeStruct((rows, width), jnp.float32)
    state_shape = jax.ShapeDtypeStruct((units, DH, DH), jnp.float32)
    work = pltpu.VMEM((2, SPAN, DH), jnp.float32)
    return pl.pallas_call(
        functools.partial(solve_kernel, count),
        grid=(units,),
        out_shape=(low_shape, low_shape, wide_shape, wide_shape, state_shape, state_shape),
        in_specs=[
            pl.BlockSpec(memory_space=pltpu.SMEM),
            pl.BlockSpec((1, 1, SPAN), lambda u: (u, 0, 0)),
            part, part, part, part, state, state,
        ],
        out_specs=(part, part, part, part, state, state),
        scratch_shapes=[
            pltpu.VMEM((SPAN, SPAN), jnp.float32),
            pltpu.VMEM((SPAN, DH), jnp.float32),
            pltpu.VMEM((3 * DH, DH), jnp.bfloat16),
            work, work, work, work,
        ],
        compiler_params=pltpu.CompilerParams(vmem_limit_bytes=WORK_BYTES),
        name="solve_blocks",
    )(ridge, gates, queries, keys, values, grads_out, gram_start, value_start)


MESH = pl.DeviceIdType.MESH


def greet(ctx_size, head_size):
    position, lane = lax.axis_index("ctx"), lax.axis_index("head")
    barrier = pltpu.get_barrier_semaphore()
    for offset in range(1, head_size):
        peer = lax.rem(lane + offset, head_size)
        pl.semaphore_signal(barrier, inc=1, device_id=(position, peer), device_id_type=MESH)
    for offset in range(1, ctx_size):
        peer = lax.rem(position + offset, ctx_size)
        pl.semaphore_signal(barrier, inc=1, device_id=(peer, lane), device_id_type=MESH)
    pl.semaphore_wait(barrier, head_size + ctx_size - 2)


def end_weights(gate_row):
    size = gate_row.shape[1]
    rowpos = lax.broadcasted_iota(jnp.int32, (size, size), 0)
    column_position = lax.broadcasted_iota(jnp.int32, (size, size), 1)
    spread = jnp.broadcast_to(gate_row, (size, size))
    return jnp.exp(jnp.sum(jnp.where(column_position > rowpos, spread, 0.0), axis=1, keepdims=True))


def log_between(totals, first, stop):
    gathered = jnp.zeros_like(totals[0])
    for index, tile in enumerate(totals):
        gathered = gathered + jnp.where(
            jnp.logical_and(index >= first, index < stop), tile, jnp.zeros_like(tile)
        )
    return gathered


def scale_heads(tile, mats, head_dev):
    return [jnp.exp(tile[u // 2 : u // 2 + 1]) * mats[u] for u in range(2 * head_dev)]


def doubling(reverse, ctx_size, head_dev, totals, mats, send_ref, slot_ref, send_sem, recv_sem):
    position, lane = lax.axis_index("ctx"), lax.axis_index("head")
    outside = [jnp.zeros((DH, DH), jnp.float32) for _ in mats]
    size, turn = 1, 0
    while size < ctx_size:
        late = lax.rem(position // size, 2)
        partner = position + size * (1 - 2 * late)
        for u, mat in enumerate(mats):
            send_ref[turn, u] = low(mat)
        copy = pltpu.make_async_remote_copy(
            src_ref=send_ref.at[turn],
            dst_ref=slot_ref.at[turn],
            send_sem=send_sem.at[turn],
            recv_sem=recv_sem.at[turn],
            device_id=(partner, lane),
            device_id_type=MESH,
        )
        copy.start()
        first = position - lax.rem(position, size)
        other = first + size * (1 - 2 * late)
        if reverse:
            takes = late == 0
            gap = log_between(totals, position + 1, first + size)
        else:
            takes = late == 1
            gap = log_between(totals, first, position)
        own_log = log_between(totals, first, first + size)
        other_log = log_between(totals, other, other + size)
        zero_log = jnp.zeros_like(own_log)
        theirs_log = jnp.where(takes, own_log, zero_log)
        mine_log = jnp.where(takes, zero_log, other_log)
        share = jnp.where(takes, 1.0, 0.0)
        copy.wait()
        theirs = [slot_ref[turn, u].astype(jnp.float32) for u in range(2 * head_dev)]
        gapped = scale_heads(gap, theirs, head_dev)
        outside = [kept + share * more for kept, more in zip(outside, gapped)]
        mats = [
            one + two
            for one, two in zip(
                scale_heads(theirs_log, theirs, head_dev), scale_heads(mine_log, mats, head_dev)
            )
        ]
        size, turn = 2 * size, turn + 1
    return outside


def exchange_kernel(
    ctx_size, head_size, gate_ref, k_in, v_in, q_in, g_in,
    k_ref, v_ref, q_ref, g_ref, gram_ref, value_ref, totals_ref,
    send_ref, slot_ref, own_sem, part_send, part_recv, total_send, total_recv, scan_send, scan_recv,
):
    position, lane = lax.axis_index("ctx"), lax.axis_index("head")
    rows, width = k_in.shape[0], k_ref.shape[1]
    units = gate_ref.shape[0]
    head_dev = width // DH
    count = units // head_dev
    greet(ctx_size, head_size)
    copies = {}
    for index, (source, target) in enumerate(((k_in, k_ref), (v_in, v_ref), (q_in, q_ref), (g_in, g_ref))):
        place = target.at[pl.ds(pl.multiple_of(lane * rows, rows), rows)]
        for offset in range(1, head_size):
            peer = lax.rem(lane + offset, head_size)
            copies[index, offset] = pltpu.make_async_remote_copy(
                src_ref=source.at[:, pl.ds(pl.multiple_of(peer * width, width), width)],
                dst_ref=place,
                send_sem=part_send.at[index, offset - 1],
                recv_sem=part_recv.at[index, offset - 1],
                device_id=(position, peer),
                device_id_type=MESH,
            )
            copies[index, offset].start()
        copies[index, 0] = pltpu.make_async_copy(
            source.at[:, pl.ds(pl.multiple_of(lane * width, width), width)], place, own_sem.at[index]
        )
        copies[index, 0].start()
    sums = [jnp.sum(gate_ref[u], axis=1, keepdims=True) for u in range(units)]
    heads = []
    for head in range(head_dev):
        total = sums[head * count]
        for block in range(1, count):
            total = total + sums[head * count + block]
        heads.append(jnp.broadcast_to(total, (1, DH)))
    heads.append(jnp.zeros((8 - head_dev, DH), jnp.float32))
    totals_ref[position] = jnp.concatenate(heads, axis=0)
    total_copies = []
    for offset in range(1, ctx_size):
        peer = lax.rem(position + offset, ctx_size)
        copy = pltpu.make_async_remote_copy(
            src_ref=totals_ref.at[position],
            dst_ref=totals_ref.at[position],
            send_sem=total_send.at[offset - 1],
            recv_sem=total_recv.at[offset - 1],
            device_id=(peer, lane),
            device_id_type=MESH,
        )
        copy.start()
        total_copies.append(copy)
    weights = [end_weights(gate_ref[u]) for u in range(units)]
    for index in (0, 1):
        copies[index, 0].wait()
        for offset in range(1, head_size):
            copies[index, offset].wait()
    mats, starts = [], []
    for head in range(head_dev):
        columns = slice(head * DH, (head + 1) * DH)
        pair = None
        for block in range(count):
            u = head * count + block
            span = slice(block * SPAN, (block + 1) * SPAN)
            keys = k_ref[span, columns]
            weighted = low(weights[u] * keys.astype(jnp.float32))
            made = (dot_tn(keys, weighted), dot_tn(v_ref[span, columns], weighted))
            if pair is None:
                pair, passed = made, sums[u]
            else:
                gram_ref[u], value_ref[u] = pair
                starts.append((u, head, passed))
                decay = jnp.exp(sums[u])
                pair = tuple(decay * old + new for old, new in zip(pair, made))
                passed = passed + sums[u]
        mats.extend(pair)
    for copy in total_copies:
        copy.wait()
    totals = [totals_ref[index] for index in range(ctx_size)]
    before = doubling(
        False, ctx_size, head_dev, totals, mats, send_ref, slot_ref, scan_send, scan_recv
    )
    for head in range(head_dev):
        gram_ref[head * count] = before[2 * head]
        value_ref[head * count] = before[2 * head + 1]
    for u, head, passed in starts:
        decay = jnp.exp(passed)
        gram_ref[u] = gram_ref[u] + decay * before[2 * head]
        value_ref[u] = value_ref[u] + decay * before[2 * head + 1]
    for index in (2, 3):
        copies[index, 0].wait()
        for offset in range(1, head_size):
            copies[index, offset].wait()


def rounds_of(ctx_size):
    return (ctx_size - 1).bit_length()


def exchange(ctx_size, head_size, gates, queries, keys, values, grads_out):
    rows, columns = queries.shape
    width = columns // head_size
    units = gates.shape[0]
    head_dev = width // DH
    rounds = rounds_of(ctx_size)
    vmem = pl.BlockSpec(memory_space=pltpu.VMEM)
    part = jax.ShapeDtypeStruct((rows * head_size, width), jnp.bfloat16)
    state = jax.ShapeDtypeStruct((units, DH, DH), jnp.float32)
    return pl.pallas_call(
        functools.partial(exchange_kernel, ctx_size, head_size),
        out_shape=(part, part, part, part, state, state, jax.ShapeDtypeStruct((ctx_size, 8, DH), jnp.float32)),
        in_specs=[vmem] * 5,
        out_specs=(vmem,) * 7,
        scratch_shapes=[
            pltpu.VMEM((rounds, 2 * head_dev, DH, DH), jnp.bfloat16),
            pltpu.VMEM((rounds, 2 * head_dev, DH, DH), jnp.bfloat16),
            pltpu.SemaphoreType.DMA((4,)),
            pltpu.SemaphoreType.DMA((4, head_size - 1)),
            pltpu.SemaphoreType.DMA((4, head_size - 1)),
            pltpu.SemaphoreType.DMA((ctx_size - 1,)),
            pltpu.SemaphoreType.DMA((ctx_size - 1,)),
            pltpu.SemaphoreType.DMA((rounds,)),
            pltpu.SemaphoreType.DMA((rounds,)),
        ],
        compiler_params=pltpu.CompilerParams(
            collective_id=0, has_side_effects=True, vmem_limit_bytes=WORK_BYTES
        ),
        name="exchange",
    )(gates, keys, values, queries, grads_out)


def finish_kernel(
    ctx_size, head_size, gate_ref, totals_ref, value_back_ref, gram_back_ref,
    part_keys_ref, part_values_ref, k_ref, v_ref, adjoint_ref,
    query_out, key_out, value_out,
    keys_ready, values_ready, send_ref, slot_ref, own_sem, part_send, part_recv, scan_send, scan_recv,
):
    position, lane = lax.axis_index("ctx"), lax.axis_index("head")
    rows, width = query_out.shape[0], k_ref.shape[1]
    units = gate_ref.shape[0]
    head_dev = width // DH
    count = units // head_dev
    greet(ctx_size, head_size)
    copies = []

    def send_back(index, source, target):
        place = target.at[:, pl.ds(pl.multiple_of(lane * width, width), width)]
        for offset in range(1, head_size):
            peer = lax.rem(lane + offset, head_size)
            copies.append(
                pltpu.make_async_remote_copy(
                    src_ref=source.at[pl.ds(pl.multiple_of(peer * rows, rows), rows)],
                    dst_ref=place,
                    send_sem=part_send.at[index, offset - 1],
                    recv_sem=part_recv.at[index, offset - 1],
                    device_id=(position, peer),
                    device_id_type=MESH,
                )
            )
            copies[-1].start()
        copies.append(
            pltpu.make_async_copy(
                source.at[pl.ds(pl.multiple_of(lane * rows, rows), rows)], place, own_sem.at[index]
            )
        )
        copies[-1].start()

    sums = [jnp.sum(gate_ref[u], axis=1, keepdims=True) for u in range(units)]
    mats = []
    for head in range(head_dev):
        last = head * count + count - 1
        pair = (value_back_ref[last], gram_back_ref[last])
        for block in reversed(range(count - 1)):
            u = head * count + block
            decay = jnp.exp(sums[u])
            pair = (decay * pair[0] + value_back_ref[u], decay * pair[1] + gram_back_ref[u])
        mats.extend(pair)
    totals = [totals_ref[index] for index in range(ctx_size)]
    after = doubling(
        True, ctx_size, head_dev, totals, mats, send_ref, slot_ref, scan_send, scan_recv
    )
    send_back(0, adjoint_ref, query_out)
    for head in range(head_dev):
        columns = slice(head * DH, (head + 1) * DH)
        value_next, gram_next = after[2 * head], after[2 * head + 1]
        for block in reversed(range(count)):
            u = head * count + block
            span = slice(block * SPAN, (block + 1) * SPAN)
            weight = end_weights(gate_ref[u])
            value_low = low(value_next)
            gram_low = low(gram_next + gram_next.T)
            keys, values = k_ref[span, columns], v_ref[span, columns]
            values_ready[span, columns] = low(
                part_values_ref[span, columns] + weight * dot_nt(keys, value_low)
            )
            keys_ready[span, columns] = low(
                part_keys_ref[span, columns]
                + weight * (dot_nn(values, value_low) + dot_nn(keys, gram_low))
            )
            decay = jnp.exp(sums[u])
            value_next = decay * value_next + value_back_ref[u]
            gram_next = decay * gram_next + gram_back_ref[u]
    send_back(1, keys_ready, key_out)
    send_back(2, values_ready, value_out)
    for copy in copies:
        copy.wait()


def finish(ctx_size, head_size, gates, totals, value_back, gram_back, part_keys, part_values, keys, values, adjoint):
    length, width = keys.shape
    rows = length // head_size
    head_dev = width // DH
    rounds = rounds_of(ctx_size)
    vmem = pl.BlockSpec(memory_space=pltpu.VMEM)
    out = jax.ShapeDtypeStruct((rows, width * head_size), jnp.bfloat16)
    return pl.pallas_call(
        functools.partial(finish_kernel, ctx_size, head_size),
        out_shape=(out, out, out),
        in_specs=[vmem] * 9,
        out_specs=(vmem,) * 3,
        scratch_shapes=[
            pltpu.VMEM((length, width), jnp.bfloat16),
            pltpu.VMEM((length, width), jnp.bfloat16),
            pltpu.VMEM((rounds, 2 * head_dev, DH, DH), jnp.bfloat16),
            pltpu.VMEM((rounds, 2 * head_dev, DH, DH), jnp.bfloat16),
            pltpu.SemaphoreType.DMA((3,)),
            pltpu.SemaphoreType.DMA((3, head_size - 1)),
            pltpu.SemaphoreType.DMA((3, head_size - 1)),
            pltpu.SemaphoreType.DMA((rounds,)),
            pltpu.SemaphoreType.DMA((rounds,)),
        ],
        compiler_params=pltpu.CompilerParams(
            collective_id=1, has_side_effects=True, vmem_limit_bytes=WORK_BYTES
        ),
        name="finish",
    )(gates, totals, value_back, gram_back, part_keys, part_values, keys, values, adjoint)


def shards(ctx_size, head_size, queries, keys, values, grads_out, log_decay, ridge):
    gates = log_decay.reshape(-1, 1, SPAN)
    keys, values, queries, grads_out, gram_start, value_start, totals = exchange(
        ctx_size, head_size, gates, queries, keys, values, grads_out
    )
    solved, adjoint, part_keys, part_values, value_back, gram_back = solve_blocks(
        ridge, gates, queries, keys, values, grads_out, gram_start, value_start
    )
    return finish(
        ctx_size, head_size, gates, totals, value_back, gram_back, part_keys, part_values, keys, values, adjoint
    )


def solution(mesh):
    return jax.shard_map(
        functools.partial(shards, mesh.shape["ctx"], mesh.shape["head"]),
        mesh=mesh,
        in_specs=(
            P(("ctx", "head"), None),
            P(("ctx", "head"), None),
            P(("ctx", "head"), None),
            P(("ctx", "head"), None),
            P("head", "ctx"),
            P("head"),
        ),
        out_specs=(P(("ctx", "head"), None), P(("ctx", "head"), None), P(("ctx", "head"), None)),
        check_vma=False,
    )
```

time: 279 us -> 124 us (0.44)
  blocking collectives: 85.6 us -> 0 us
  waiting for transfers between devices: 73.2 us -> 0 us
  Pallas kernels: 41.9 us -> 114 us
  starting transfers between devices: 25.4 us -> 0 us
  between operations: 15.1 us -> 0.67 us
  local copies, waits for them, and re-layouts: 20 us -> 9.13 us
  other arithmetic: 10.8 us -> 0 us
  matrix products: 5.76 us -> 0 us
    pallas_call x0 -> x2, Pallas kernels: none -> 72.3 us  [the longest x1 36.3 us: finish(): pl.pallas_call(functools.partial(finish_kernel, ctx_size, head_size), out...]
    all_gather x2 -> x0, blocking collectives: 63.2 us -> none  [the longest x1 31.9 us: shards(): lax.all_gather(value_delta[None].astype(jnp.bfloat16), 'ctx', axis=0, til...]
    all_gather x2 -> x0, waiting for transfers between devices: 46.1 us -> none  [the longest x1 41.1 us: shards(): lax.all_gather(value_carry[None], 'ctx', axis=0, tiled=True)]
    all_to_all x7 -> x0, waiting for transfers between devices: 27.1 us -> none  [the longest x1 7.97 us: shards(): lax.all_to_all(values, 'head', split_axis=1, concat_axis=0, tiled=True)]
    all_to_all x7 -> x0, starting transfers between devices: 25.4 us -> none  [the longest x1 4.37 us: shards(): lax.all_to_all(keys, 'head', split_axis=1, concat_axis=0, tiled=True)]
    unnamed x1 -> x0, blocking collectives: 22.4 us -> none
    all_to_all x7 -> x0, local copies, waits for them, and re-layouts: 6.93 us -> none  [the longest x1 1.87 us: shards(): lax.all_to_all(keys, 'head', split_axis=1, concat_axis=0, tiled=True)]
    dot_general x7 -> x0, matrix products: 5.76 us -> none  [the longest x1 1.33 us: shards(): jnp.einsum('hnck,hncl->hnkl', key_wide, scaled_lookup_vectors, precision=...]
  transfers between devices with their start and end apart: 9 -> 0, of which waited for: 6 -> 0; matrix products, arithmetic and copies ran while one was open for 8% -> 0% of each run, Pallas kernels for 0% -> 0%
where the time goes in v2:
time: 124 us
  Pallas kernels  114 us (92%)
  local copies, waits for them, and re-layouts  9.13 us (7%)
    pallas_call x1, Pallas kernels, solve_blocks(): pl.pallas_call(functools.partial(solve_kernel, count), grid=(units,), out...  42 us
    pallas_call x1, Pallas kernels, finish(): pl.pallas_call(functools.partial(finish_kernel, ctx_size, head_size), out...  36.3 us
    pallas_call x1, Pallas kernels, exchange(): pl.pallas_call(functools.partial(exchange_kernel, ctx_size, head_size), o...  36 us
    unnamed x15, local copies, waits for them, and re-layouts  8.42 us

profile of v2, /device:TPU:0, one launch (start us, length us, event | category | flops | bytes accessed | tf_op | source)
XLA Modules:
  0.0 124.0 jit_solution(18419852100742282685)
XLA Ops:
  0.6 0.7 reshape.9.gate_ref
  1.3 0.0 copy-start.1
  1.4 1.0 copy-done.1
  2.4 0.0 copy-start.2
  2.4 1.0 copy-done.2
  3.4 0.0 copy-start.3
  3.4 1.0 copy-done.3
  4.5 0.0 copy-start.4
  4.5 1.0 copy-done.4
  5.5 36.0 %exchange.1 = (bf16[1024,256]{1,0:T(8,128)(2,1)S(1)}, bf16[1024,256]{1,0:T(8,128)(2,1)S(1)}, bf16[1024,256]{1,0:T(8,128)(2,1)S(1)}, bf16[1024,256]{1,0:T(8,128)(...) custom-call(f32[4,1,512]{2,1,0:T(1,128)S(1)} %reshape.9.gate_ref, ...), custom_call_target="tpu_custom_call" | custom-call | tf_op jit(solution)/shard_map/exchange/pallas_call | solution.py:355
  41.5 0.0 copy-start.5
  41.5 0.6 copy-done.5
  42.1 42.0 %solve_blocks.1 = (bf16[1024,256]{1,0:T(8,128)(2,1)}, bf16[1024,256]{1,0:T(8,128)(2,1)S(1)}, f32[1024,256]{1,0:T(8,128)S(1)}, f32[1024,256]{1,0:T(8,128)}, f32[4...) custom-call(f32[2]{0:T(128)S(1)} %copy-done.5, f32[4,1,512]{2,1,0:T(1,128)S(1)} %reshape.9.gate_ref, ...), custom_call_target="tpu_custom_call" | custom-call | tf_op jit(solution)/shard_map/solve_blocks/pallas_call | solution.py:145
  84.1 0.0 copy-start
  84.1 1.2 copy-done
  85.4 36.3 %finish.1 = (bf16[256,1024]{1,0:T(8,128)(2,1)S(1)}, bf16[256,1024]{1,0:T(8,128)(2,1)S(1)}, bf16[256,1024]{1,0:T(8,128)(2,1)S(1)}) custom-call(f32[4,1,512]{2,1,0:T(1,128)S(1)} %reshape.9.gate_ref, f32[8,8,128]{2,1,0:T(8,128)S(1)} %get-tuple-element.15.totals_ref, f32[4,128,128]{2,1,0:T(8,128)S(1)} %get-tuple-element.22.value_back_ref, ...), custom_call_target="tpu_custom_call" | custom-call | tf_op jit(solution)/shard_map/finish/pallas_call | solution.py:462
  121.7 0.8 copy.12
  122.5 0.8 copy.13
  123.3 0.8 copy.14
Async XLA Ops:
  1.3 1.0 copy-start.1
  2.4 1.0 copy-start.2
  3.4 1.0 copy-start.3
  4.5 1.0 copy-start.4
  41.5 0.7 copy-start.5
  84.1 1.2 copy-start

commit v3 on v2

--- a/solution.py
+++ b/solution.py
@@ -66,8 +66,7 @@
     decay_ref[...] = jnp.broadcast_to(jnp.exp(column), decay_ref.shape)
     gram_high, gram_low = two_parts(gram_ref[0])
     stack_ref[0:DH] = gram_high
-    stack_ref[DH : 2 * DH] = gram_high
-    stack_ref[2 * DH : 3 * DH] = gram_low
+    stack_ref[DH : 2 * DH] = gram_low
     value_high, value_low = two_parts(value_ref[0])
     span = q_ref.shape[0]
     chunks = [(start, start + CHUNK) for start in range(0, span, CHUNK)]
@@ -90,10 +89,10 @@
             rows = slice(start, stop)
             for side in range(2):
                 direction = p_ref[side, rows]
-                high, rest = two_parts(direction)
+                high = low(direction)
                 scores = low(within_ref[rows, 0:stop] * dot_nt(high, k_ref[0:stop]))
                 image = (
-                    decay_ref[rows] * dot_nn(jnp.concatenate([high, rest, high], axis=1), stack_ref[...])
+                    decay_ref[rows] * dot_nn(jnp.concatenate([high, high], axis=1), stack_ref[...])
                     + dot_nn(scores, k_ref[0:stop])
                     + ridge * direction
                 )
@@ -155,7 +154,7 @@
         scratch_shapes=[
             pltpu.VMEM((SPAN, SPAN), jnp.float32),
             pltpu.VMEM((SPAN, DH), jnp.float32),
-            pltpu.VMEM((3 * DH, DH), jnp.bfloat16),
+            pltpu.VMEM((2 * DH, DH), jnp.bfloat16),
             work, work, work, work,
         ],
         compiler_params=pltpu.CompilerParams(vmem_limit_bytes=WORK_BYTES),
@@ -199,7 +198,9 @@
     return [jnp.exp(tile[u // 2 : u // 2 + 1]) * mats[u] for u in range(2 * head_dev)]
 
 
-def doubling(reverse, ctx_size, head_dev, totals, mats, send_ref, slot_ref, send_sem, recv_sem):
+def doubling(
+    reverse, ctx_size, head_dev, totals, mats, send_ref, slot_ref, send_sem, recv_sem, meanwhile=None
+):
     position, lane = lax.axis_index("ctx"), lax.axis_index("head")
     outside = [jnp.zeros((DH, DH), jnp.float32) for _ in mats]
     size, turn = 1, 0
@@ -231,6 +232,8 @@
         theirs_log = jnp.where(takes, own_log, zero_log)
         mine_log = jnp.where(takes, zero_log, other_log)
         share = jnp.where(takes, 1.0, 0.0)
+        if meanwhile is not None and turn == 0:
+            meanwhile()
         copy.wait()
         theirs = [slot_ref[turn, u].astype(jnp.float32) for u in range(2 * head_dev)]
         gapped = scale_heads(gap, theirs, head_dev)
@@ -355,7 +358,7 @@
     return pl.pallas_call(
         functools.partial(exchange_kernel, ctx_size, head_size),
         out_shape=(part, part, part, part, state, state, jax.ShapeDtypeStruct((ctx_size, 8, DH), jnp.float32)),
-        in_specs=[vmem] * 5,
+        in_specs=[vmem] + [pl.BlockSpec(memory_space=pl.ANY)] * 4,
         out_specs=(vmem,) * 7,
         scratch_shapes=[
             pltpu.VMEM((rounds, 2 * head_dev, DH, DH), jnp.bfloat16),
@@ -422,32 +425,35 @@
             pair = (decay * pair[0] + value_back_ref[u], decay * pair[1] + gram_back_ref[u])
         mats.extend(pair)
     totals = [totals_ref[index] for index in range(ctx_size)]
+    weights = []
+
+    def meanwhile():
+        send_back(0, adjoint_ref, query_out)
+        weights.extend(end_weights(gate_ref[u]) for u in range(units))
+
     after = doubling(
-        True, ctx_size, head_dev, totals, mats, send_ref, slot_ref, scan_send, scan_recv
+        True, ctx_size, head_dev, totals, mats, send_ref, slot_ref, scan_send, scan_recv, meanwhile
     )
-    send_back(0, adjoint_ref, query_out)
+    states = []
     for head in range(head_dev):
         columns = slice(head * DH, (head + 1) * DH)
         value_next, gram_next = after[2 * head], after[2 * head + 1]
         for block in reversed(range(count)):
             u = head * count + block
             span = slice(block * SPAN, (block + 1) * SPAN)
-            weight = end_weights(gate_ref[u])
             value_low = low(value_next)
-            gram_low = low(gram_next + gram_next.T)
-            keys, values = k_ref[span, columns], v_ref[span, columns]
             values_ready[span, columns] = low(
-                part_values_ref[span, columns] + weight * dot_nt(keys, value_low)
+                part_values_ref[span, columns] + weights[u] * dot_nt(k_ref[span, columns], value_low)
             )
-            keys_ready[span, columns] = low(
-                part_keys_ref[span, columns]
-                + weight * (dot_nn(values, value_low) + dot_nn(keys, gram_low))
-            )
+            states.append((u, span, columns, value_low, low(gram_next + gram_next.T)))
             decay = jnp.exp(sums[u])
             value_next = decay * value_next + value_back_ref[u]
             gram_next = decay * gram_next + gram_back_ref[u]
-    send_back(1, keys_ready, key_out)
-    send_back(2, values_ready, value_out)
+    send_back(1, values_ready, value_out)
+    for u, span, columns, value_low, gram_low in states:
+        added = dot_nn(v_ref[span, columns], value_low) + dot_nn(k_ref[span, columns], gram_low)
+        keys_ready[span, columns] = low(part_keys_ref[span, columns] + weights[u] * added)
+    send_back(2, keys_ready, key_out)
     for copy in copies:
         copy.wait()
 

time: 124 us -> 119 us (0.960)
  Pallas kernels: 114 us -> 109 us
    pallas_call x1, Pallas kernels: 36.3 us -> 31 us  [finish(): pl.pallas_call(functools.partial(finish_kernel, ctx_size, head_size), out...]
where the time goes in v3:
time: 119 us; the launch traced here: 118 us
  Pallas kernels  109 us (92%)
  local copies, waits for them, and re-layouts  9.13 us (8%)
    pallas_call x1, Pallas kernels, solve_blocks(): pl.pallas_call(functools.partial(solve_kernel, count), grid=(units,), out...  41.6 us
    pallas_call x1, Pallas kernels, exchange(): pl.pallas_call(functools.partial(exchange_kernel, ctx_size, head_size), o...  36 us
    pallas_call x1, Pallas kernels, finish(): pl.pallas_call(functools.partial(finish_kernel, ctx_size, head_size), out...  31 us
    unnamed x15, local copies, waits for them, and re-layouts  8.42 us

profile of v3, /device:TPU:0, one launch (start us, length us, event | category | flops | bytes accessed | tf_op | source)
XLA Modules:
  0.0 118.4 jit_solution(11430409757326069076)
XLA Ops:
  0.6 0.7 reshape.9.gate_ref
  1.3 0.0 copy-start.1
  1.4 1.0 copy-done.1
  2.4 0.0 copy-start.2
  2.4 1.0 copy-done.2
  3.4 0.0 copy-start.3
  3.4 1.0 copy-done.3
  4.5 0.0 copy-start.4
  4.5 1.0 copy-done.4
  5.5 36.0 %exchange.1 = (bf16[1024,256]{1,0:T(8,128)(2,1)S(1)}, bf16[1024,256]{1,0:T(8,128)(2,1)S(1)}, bf16[1024,256]{1,0:T(8,128)(2,1)S(1)}, bf16[1024,256]{1,0:T(8,128)(...) custom-call(f32[4,1,512]{2,1,0:T(1,128)S(1)} %reshape.9.gate_ref, ...), custom_call_target="tpu_custom_call" | custom-call | tf_op jit(solution)/shard_map/exchange/pallas_call | solution.py:358
  41.5 0.0 copy-start.5
  41.5 0.6 copy-done.5
  42.1 41.6 %solve_blocks.1 = (bf16[1024,256]{1,0:T(8,128)(2,1)}, bf16[1024,256]{1,0:T(8,128)(2,1)S(1)}, f32[1024,256]{1,0:T(8,128)S(1)}, f32[1024,256]{1,0:T(8,128)}, f32[4...) custom-call(f32[2]{0:T(128)S(1)} %copy-done.5, f32[4,1,512]{2,1,0:T(1,128)S(1)} %reshape.9.gate_ref, ...), custom_call_target="tpu_custom_call" | custom-call | tf_op jit(solution)/shard_map/solve_blocks/pallas_call | solution.py:144
  83.7 0.0 copy-start
  83.7 1.2 %copy-done = f32[1024,256]{1,0:T(8,128)S(1)} copy-done((f32[1024,256]{1,0:T(8,128)S(1)}, f32[1024,256]{1,0:T(8,128)}, u32[]{:S(2)}) %copy-start) | copy-done | bytes 1048600
  85.0 31.0 %finish.1 = (bf16[256,1024]{1,0:T(8,128)(2,1)S(1)}, bf16[256,1024]{1,0:T(8,128)(2,1)S(1)}, bf16[256,1024]{1,0:T(8,128)(2,1)S(1)}) custom-call(f32[4,1,512]{2,1,0:T(1,128)S(1)} %reshape.9.gate_ref, f32[8,8,128]{2,1,0:T(8,128)S(1)} %get-tuple-element.15.totals_ref, f32[4,128,128]{2,1,0:T(8,128)S(1)} %get-tuple-element.22.value_back_ref, ...), custom_call_target="tpu_custom_call" | custom-call | tf_op jit(solution)/shard_map/finish/pallas_call | solution.py:468
  116.0 0.8 copy.12
  116.8 0.8 copy.13
  117.6 0.8 copy.14
Async XLA Ops:
  1.3 1.0 copy-start.1
  2.4 1.0 copy-start.2
  3.4 1.0 copy-start.3
  4.5 1.0 copy-start.4
  41.5 0.7 copy-start.5
  83.7 1.2 %copy-start = (f32[1024,256]{1,0:T(8,128)S(1)}, f32[1024,256]{1,0:T(8,128)}, u32[]{:S(2)}) copy-start(f32[1024,256]{1,0:T(8,128)} %get-tuple-element.25.part_values_ref) | copy-start | bytes 3145732
